TPU v7x, 32 devices: a whole 2x2x4 slice. The times are simulated.
32 devices in a mesh: mesh: 8 (over z, x), sub: 4 (over y, core).
Axes of the slice: x: 2, y: 2, z: 4, core: 2. Of those that a mesh axis runs over, the one named last changes fastest.
Arguments:
- conductivity: float32 [4, 32, 2, 64, 128], P('sub', 'mesh'), may hold values from 0.3 to 3
- footprint: int32 [8, 8], replicated, may hold values from 0 to 31, as said below
- initial: float32 [8, 8, 512, 128], P('mesh', 'sub'), may hold values from -30 to 30
- observed: float32 [8, 3, 8, 512, 128], P('mesh', None, 'sub'), may hold values from -6 to 6
Outputs:
- gradient: float32 [4, 32, 2, 64, 128], P('sub', 'mesh')
- last_field: float32 [8, 8, 512, 128], P('mesh', 'sub')
Inputs may be any that keep to these rules, and one draw needn't show every extreme that they name: `footprint`: each row names 8 different blocks; in every row, each range k * 4 to (k + 1) * 4 - 1 holds at most one of the row's ids.
All inputs are finite; a program needn't handle non-finite values.
Results may differ from a plain program's by a relative error of at most 0.00011.
Values sent between devices are 32-bit elements; how exact they have to be, the bound alone decides.
A program may use at most 128 MiB of HBM per device.

v0:
```python
import jax
import jax.numpy as jnp
from jax import lax
from jax.sharding import PartitionSpec as P

STEPS = 3
DEG = 6


low_bound = 0.3
high_bound = 15.0


def padded_2(x, sides, width):
    for axis, dim in sides:
        count, length = (lax.axis_size(axis), x.shape[dim])
        up = [(i, (i + 1) % count) for i in range(count - 1)]
        down = [(j, i) for i, j in up]
        last = lax.slice_in_dim(x, length - width, length, axis=dim)
        leading = lax.slice_in_dim(x, 0, width, axis=dim)
        before = lax.ppermute(last, axis, up)
        after = lax.ppermute(leading, axis, down)
        x = jnp.concatenate([before, x, after], axis=dim)
    return x


def halo_operator(field, conduct):
    padded = padded_2(field, (("sub", 0),), 1)
    padded = jnp.pad(padded, ((0, 0), (1, 1), (1, 1)))
    beside = padded[2:, 1:-1, 1:-1] + padded[:-2, 1:-1, 1:-1]
    beside = beside + padded[1:-1, 2:, 1:-1] + padded[1:-1, :-2, 1:-1]
    beside = beside + padded[1:-1, 1:-1, 2:] + padded[1:-1, 1:-1, :-2]
    return (6.0 + conduct) * field - beside


def chebyshev(source, conduct, operate):
    centre = (high_bound + low_bound) / 2.0
    half_width = (high_bound - low_bound) / 2.0
    ratio_now = half_width / centre
    direct = source / centre
    remain = source
    iterate = direct
    for repeat in range(DEG):
        remain = remain - operate(direct, conduct)
        ratio_next = 1.0 / (2.0 * centre / half_width - ratio_now)
        direct = ratio_next * ratio_now * direct + 2.0 * ratio_next / half_width * remain
        iterate = iterate + direct
        ratio_now = ratio_next
    return iterate


def one_mesh(conduct, start_field, observed_mesh, operate):
    fields = [start_field]
    for step in range(STEPS):
        fields.append(chebyshev(conduct * fields[-1], conduct, operate))
    adjoint = jnp.zeros_like(start_field)
    summed = jnp.zeros_like(start_field)
    for step in range(STEPS, 0, -1):
        adjoint = chebyshev(
            fields[step] - observed_mesh[step - 1] + conduct * adjoint, conduct, operate
        )
        summed = summed + adjoint * (fields[step - 1] - fields[step])
    return (fields[-1], summed)


def body(conductivity, footprint, initial, observed):
    my_index = lax.axis_index("mesh")
    per_owner = conductivity.shape[1]
    depth = conductivity.shape[2]
    block_y = conductivity.shape[3]
    across = conductivity.shape[4]
    tile_count = footprint.shape[1]
    cell_count = depth * block_y * across
    my_blocks = lax.dynamic_index_in_dim(footprint, my_index, 0, keepdims=False)
    shard_rows = lax.all_gather(conductivity, "mesh", axis=1, tiled=True)
    row_count = shard_rows.shape[1]
    flat_rows = shard_rows[0].reshape(row_count, cell_count)
    chosen = (my_blocks[:, None] == jnp.arange(row_count, dtype=jnp.int32)[None, :]).astype(
        jnp.float32
    )
    tile_values = jnp.dot(chosen, flat_rows, precision=lax.Precision.HIGHEST)
    conduct = jnp.transpose(
        tile_values.reshape(tile_count, depth, block_y, across), (1, 0, 2, 3)
    ).reshape(depth, tile_count * block_y, across)
    final_field, summed = one_mesh(conduct, initial[0], observed[0], halo_operator)
    grad_tiles = jnp.transpose(
        summed.reshape(depth, tile_count, block_y, across), (1, 0, 2, 3)
    ).reshape(tile_count, cell_count)
    chosen = (
        jnp.arange(per_owner * lax.axis_size("mesh"), dtype=jnp.int32)[:, None]
        == my_blocks[None, :]
    ).astype(jnp.float32)
    grad_rows = lax.psum_scatter(
        jnp.dot(chosen, grad_tiles, precision=lax.Precision.HIGHEST),
        "mesh",
        scatter_dimension=0,
        tiled=True,
    )
    gradient = grad_rows.reshape(1, per_owner, depth, block_y, across)
    return (gradient, final_field[None])


def solution(mesh):
    return jax.shard_map(
        body,
        mesh=mesh,
        in_specs=(
            P("sub", "mesh", None, None, None),
            P(),
            P("mesh", "sub", None, None),
            P("mesh", None, "sub", None, None),
        ),
        out_specs=(P("sub", "mesh", None, None, None), P("mesh", "sub", None, None)),
        check_vma=False,
    )
```

profile of v0, /device:TPU:0, one launch (start us, length us, event | category | flops | bytes accessed | tf_op | source)
XLA Modules:
  0.0 570.6 jit_solution(3698757126698177843)
XLA Ops:
  8.0 54.2 %all-gather.2.cloned.1.call-done = f32[1,32,2,64,128]{4,3,2,0,1:T(8,128)} async-done(((f32[1,4,2,64,128]{4,3,2,0,1:T(8,128)}), f32[1,32,2,64,128]{4,3,2,0,1:T(8,128)}) %all-gather.2.cloned.1.call-update) | async-done | bytes 2097168 | tf_op jit(solution)/shard_map/all_gather | solution.py:75
  62.2 2.8 copy.27
  65.4 2.0 fusion.5
  67.6 1.3 collective-permute-start
  68.9 3.0 collective-permute-start.1
  74.3 1.3 collective-permute-start.2
  75.6 5.8 %collective-permute-start.3 = (f32[1,512,128]{2,1,0:T(8,128)S(1)}, f32[1,512,128]{2,1,0:T(8,128)S(1)}, u32[]{:S(2)}, u32[]{:S(2)}) collective-permute-start(f32[1,512,128]{2,1,0:T(8,128)S(1)} %get-tuple-element.147), channel_id=1, source_target_pairs={{0,1},{1,2},{2,3},{4,5},{5,6},{6,7},{8,9},{9,10},{10,11},{12,13},{... | collective-permute-start | bytes 786440 | tf_op jit(solution)/shard_map/ppermute | solution.py:21
  83.7 1.3 collective-permute-start.4
  85.0 7.2 %collective-permute-start.5 = (f32[1,512,128]{2,1,0:T(8,128)S(1)}, f32[1,512,128]{2,1,0:T(8,128)S(1)}, u32[]{:S(2)}, u32[]{:S(2)}) collective-permute-start(f32[1,512,128]{2,1,0:T(8,128)S(1)} %get-tuple-element.145), channel_id=1, source_target_pairs={{0,1},{1,2},{2,3},{4,5},{5,6},{6,7},{8,9},{9,10},{10,11},{12,13},{... | collective-permute-start | bytes 786440 | tf_op jit(solution)/shard_map/ppermute | solution.py:21
  94.6 1.3 collective-permute-start.6
  95.9 7.2 %collective-permute-start.7 = (f32[1,512,128]{2,1,0:T(8,128)S(1)}, f32[1,512,128]{2,1,0:T(8,128)S(1)}, u32[]{:S(2)}, u32[]{:S(2)}) collective-permute-start(f32[1,512,128]{2,1,0:T(8,128)S(1)} %get-tuple-element.143), channel_id=1, source_target_pairs={{0,1},{1,2},{2,3},{4,5},{5,6},{6,7},{8,9},{9,10},{10,11},{12,13},{... | collective-permute-start | bytes 786440 | tf_op jit(solution)/shard_map/ppermute | solution.py:21
  105.4 1.3 collective-permute-start.8
  106.7 7.2 %collective-permute-start.9 = (f32[1,512,128]{2,1,0:T(8,128)S(1)}, f32[1,512,128]{2,1,0:T(8,128)S(1)}, u32[]{:S(2)}, u32[]{:S(2)}) collective-permute-start(f32[1,512,128]{2,1,0:T(8,128)S(1)} %get-tuple-element.141), channel_id=1, source_target_pairs={{0,1},{1,2},{2,3},{4,5},{5,6},{6,7},{8,9},{9,10},{10,11},{12,13},{... | collective-permute-start | bytes 786440 | tf_op jit(solution)/shard_map/ppermute | solution.py:21
  116.2 1.3 collective-permute-start.10
  117.5 7.6 %collective-permute-start.11 = (f32[1,512,128]{2,1,0:T(8,128)S(1)}, f32[1,512,128]{2,1,0:T(8,128)S(1)}, u32[]{:S(2)}, u32[]{:S(2)}) collective-permute-start(f32[1,512,128]{2,1,0:T(8,128)S(1)} %get-tuple-element.139), channel_id=1, source_target_pairs={{0,1},{1,2},{2,3},{4,5},{5,6},{6,7},{8,9},{9,10},{10,11},{12,13},{... | collective-permute-start | bytes 786440 | tf_op jit(solution)/shard_map/ppermute | solution.py:21
  127.2 1.3 collective-permute-start.12
  128.5 7.2 %collective-permute-start.13 = (f32[1,512,128]{2,1,0:T(8,128)S(1)}, f32[1,512,128]{2,1,0:T(8,128)S(1)}, u32[]{:S(2)}, u32[]{:S(2)}) collective-permute-start(f32[1,512,128]{2,1,0:T(8,128)S(1)} %get-tuple-element.137), channel_id=1, source_target_pairs={{0,1},{1,2},{2,3},{4,5},{5,6},{6,7},{8,9},{9,10},{10,11},{12,13},{... | collective-permute-start | bytes 786440 | tf_op jit(solution)/shard_map/ppermute | solution.py:21
  138.0 1.3 collective-permute-start.14
  139.3 7.2 %collective-permute-start.15 = (f32[1,512,128]{2,1,0:T(8,128)S(1)}, f32[1,512,128]{2,1,0:T(8,128)S(1)}, u32[]{:S(2)}, u32[]{:S(2)}) collective-permute-start(f32[1,512,128]{2,1,0:T(8,128)S(1)} %get-tuple-element.135), channel_id=1, source_target_pairs={{0,1},{1,2},{2,3},{4,5},{5,6},{6,7},{8,9},{9,10},{10,11},{12,13},{... | collective-permute-start | bytes 786440 | tf_op jit(solution)/shard_map/ppermute | solution.py:21
  148.8 1.3 collective-permute-start.16
  150.1 7.2 %collective-permute-start.17 = (f32[1,512,128]{2,1,0:T(8,128)S(1)}, f32[1,512,128]{2,1,0:T(8,128)S(1)}, u32[]{:S(2)}, u32[]{:S(2)}) collective-permute-start(f32[1,512,128]{2,1,0:T(8,128)S(1)} %get-tuple-element.133), channel_id=1, source_target_pairs={{0,1},{1,2},{2,3},{4,5},{5,6},{6,7},{8,9},{9,10},{10,11},{12,13},{... | collective-permute-start | bytes 786440 | tf_op jit(solution)/shard_map/ppermute | solution.py:21
  159.6 1.3 collective-permute-start.18
  160.9 7.2 %collective-permute-start.19 = (f32[1,512,128]{2,1,0:T(8,128)S(1)}, f32[1,512,128]{2,1,0:T(8,128)S(1)}, u32[]{:S(2)}, u32[]{:S(2)}) collective-permute-start(f32[1,512,128]{2,1,0:T(8,128)S(1)} %get-tuple-element.131), channel_id=1, source_target_pairs={{0,1},{1,2},{2,3},{4,5},{5,6},{6,7},{8,9},{9,10},{10,11},{12,13},{... | collective-permute-start | bytes 786440 | tf_op jit(solution)/shard_map/ppermute | solution.py:21
  170.5 1.3 collective-permute-start.20
  171.8 7.2 %collective-permute-start.21 = (f32[1,512,128]{2,1,0:T(8,128)S(1)}, f32[1,512,128]{2,1,0:T(8,128)S(1)}, u32[]{:S(2)}, u32[]{:S(2)}) collective-permute-start(f32[1,512,128]{2,1,0:T(8,128)S(1)} %get-tuple-element.129), channel_id=1, source_target_pairs={{0,1},{1,2},{2,3},{4,5},{5,6},{6,7},{8,9},{9,10},{10,11},{12,13},{... | collective-permute-start | bytes 786440 | tf_op jit(solution)/shard_map/ppermute | solution.py:21
  181.3 1.3 collective-permute-start.22
  182.6 7.2 %collective-permute-start.23 = (f32[1,512,128]{2,1,0:T(8,128)S(1)}, f32[1,512,128]{2,1,0:T(8,128)S(1)}, u32[]{:S(2)}, u32[]{:S(2)}) collective-permute-start(f32[1,512,128]{2,1,0:T(8,128)S(1)} %get-tuple-element.127), channel_id=1, source_target_pairs={{0,1},{1,2},{2,3},{4,5},{5,6},{6,7},{8,9},{9,10},{10,11},{12,13},{... | collective-permute-start | bytes 786440 | tf_op jit(solution)/shard_map/ppermute | solution.py:21
  192.3 1.3 collective-permute-start.24
  193.6 7.2 %collective-permute-start.25 = (f32[1,512,128]{2,1,0:T(8,128)S(1)}, f32[1,512,128]{2,1,0:T(8,128)S(1)}, u32[]{:S(2)}, u32[]{:S(2)}) collective-permute-start(f32[1,512,128]{2,1,0:T(8,128)S(1)} %get-tuple-element.125), channel_id=1, source_target_pairs={{0,1},{1,2},{2,3},{4,5},{5,6},{6,7},{8,9},{9,10},{10,11},{12,13},{... | collective-permute-start | bytes 786440 | tf_op jit(solution)/shard_map/ppermute | solution.py:21
  203.1 1.3 collective-permute-start.26
  204.4 7.4 %collective-permute-start.27 = (f32[1,512,128]{2,1,0:T(8,128)S(1)}, f32[1,512,128]{2,1,0:T(8,128)S(1)}, u32[]{:S(2)}, u32[]{:S(2)}) collective-permute-start(f32[1,512,128]{2,1,0:T(8,128)S(1)} %get-tuple-element.123), channel_id=1, source_target_pairs={{0,1},{1,2},{2,3},{4,5},{5,6},{6,7},{8,9},{9,10},{10,11},{12,13},{... | collective-permute-start | bytes 786440 | tf_op jit(solution)/shard_map/ppermute | solution.py:21
  213.9 1.3 collective-permute-start.28
  215.2 7.2 %collective-permute-start.29 = (f32[1,512,128]{2,1,0:T(8,128)S(1)}, f32[1,512,128]{2,1,0:T(8,128)S(1)}, u32[]{:S(2)}, u32[]{:S(2)}) collective-permute-start(f32[1,512,128]{2,1,0:T(8,128)S(1)} %get-tuple-element.121), channel_id=1, source_target_pairs={{0,1},{1,2},{2,3},{4,5},{5,6},{6,7},{8,9},{9,10},{10,11},{12,13},{... | collective-permute-start | bytes 786440 | tf_op jit(solution)/shard_map/ppermute | solution.py:21
  224.8 1.3 collective-permute-start.30
  226.1 7.2 %collective-permute-start.31 = (f32[1,512,128]{2,1,0:T(8,128)S(1)}, f32[1,512,128]{2,1,0:T(8,128)S(1)}, u32[]{:S(2)}, u32[]{:S(2)}) collective-permute-start(f32[1,512,128]{2,1,0:T(8,128)S(1)} %get-tuple-element.119), channel_id=1, source_target_pairs={{0,1},{1,2},{2,3},{4,5},{5,6},{6,7},{8,9},{9,10},{10,11},{12,13},{... | collective-permute-start | bytes 786440 | tf_op jit(solution)/shard_map/ppermute | solution.py:21
  235.6 1.3 collective-permute-start.32
  236.9 7.2 %collective-permute-start.33 = (f32[1,512,128]{2,1,0:T(8,128)S(1)}, f32[1,512,128]{2,1,0:T(8,128)S(1)}, u32[]{:S(2)}, u32[]{:S(2)}) collective-permute-start(f32[1,512,128]{2,1,0:T(8,128)S(1)} %get-tuple-element.117), channel_id=1, source_target_pairs={{0,1},{1,2},{2,3},{4,5},{5,6},{6,7},{8,9},{9,10},{10,11},{12,13},{... | collective-permute-start | bytes 786440 | tf_op jit(solution)/shard_map/ppermute | solution.py:21
  246.4 1.4 collective-permute-start.34
  247.8 7.2 %collective-permute-start.35 = (f32[1,512,128]{2,1,0:T(8,128)S(1)}, f32[1,512,128]{2,1,0:T(8,128)S(1)}, u32[]{:S(2)}, u32[]{:S(2)}) collective-permute-start(f32[1,512,128]{2,1,0:T(8,128)S(1)} %get-tuple-element.115), channel_id=1, source_target_pairs={{0,1},{1,2},{2,3},{4,5},{5,6},{6,7},{8,9},{9,10},{10,11},{12,13},{... | collective-permute-start | bytes 786440 | tf_op jit(solution)/shard_map/ppermute | solution.py:21
  257.5 1.3 collective-permute-start.36
  258.8 7.2 %collective-permute-start.37 = (f32[1,512,128]{2,1,0:T(8,128)S(1)}, f32[1,512,128]{2,1,0:T(8,128)S(1)}, u32[]{:S(2)}, u32[]{:S(2)}) collective-permute-start(f32[1,512,128]{2,1,0:T(8,128)S(1)} %get-tuple-element.113), channel_id=1, source_target_pairs={{0,1},{1,2},{2,3},{4,5},{5,6},{6,7},{8,9},{9,10},{10,11},{12,13},{... | collective-permute-start | bytes 786440 | tf_op jit(solution)/shard_map/ppermute | solution.py:21
  269.7 7.2 %collective-permute-start.39 = (f32[1,512,128]{2,1,0:T(8,128)S(1)}, f32[1,512,128]{2,1,0:T(8,128)S(1)}, u32[]{:S(2)}, u32[]{:S(2)}) collective-permute-start(f32[1,512,128]{2,1,0:T(8,128)S(1)} %get-tuple-element.111), channel_id=1, source_target_pairs={{0,1},{1,2},{2,3},{4,5},{5,6},{6,7},{8,9},{9,10},{10,11},{12,13},{... | collective-permute-start | bytes 786440 | tf_op jit(solution)/shard_map/ppermute | solution.py:21
  280.5 7.2 %collective-permute-start.41 = (f32[1,512,128]{2,1,0:T(8,128)S(1)}, f32[1,512,128]{2,1,0:T(8,128)S(1)}, u32[]{:S(2)}, u32[]{:S(2)}) collective-permute-start(f32[1,512,128]{2,1,0:T(8,128)S(1)} %get-tuple-element.109), channel_id=1, source_target_pairs={{0,1},{1,2},{2,3},{4,5},{5,6},{6,7},{8,9},{9,10},{10,11},{12,13},{... | collective-permute-start | bytes 786440 | tf_op jit(solution)/shard_map/ppermute | solution.py:21
  291.3 7.4 %collective-permute-start.43 = (f32[1,512,128]{2,1,0:T(8,128)S(1)}, f32[1,512,128]{2,1,0:T(8,128)S(1)}, u32[]{:S(2)}, u32[]{:S(2)}) collective-permute-start(f32[1,512,128]{2,1,0:T(8,128)S(1)} %get-tuple-element.107), channel_id=1, source_target_pairs={{0,1},{1,2},{2,3},{4,5},{5,6},{6,7},{8,9},{9,10},{10,11},{12,13},{... | collective-permute-start | bytes 786440 | tf_op jit(solution)/shard_map/ppermute | solution.py:21
  302.1 7.2 %collective-permute-start.45 = (f32[1,512,128]{2,1,0:T(8,128)S(1)}, f32[1,512,128]{2,1,0:T(8,128)S(1)}, u32[]{:S(2)}, u32[]{:S(2)}) collective-permute-start(f32[1,512,128]{2,1,0:T(8,128)S(1)} %get-tuple-element.105), channel_id=1, source_target_pairs={{0,1},{1,2},{2,3},{4,5},{5,6},{6,7},{8,9},{9,10},{10,11},{12,13},{... | collective-permute-start | bytes 786440 | tf_op jit(solution)/shard_map/ppermute | solution.py:21
  311.6 1.3 collective-permute-start.46
  312.9 7.2 %collective-permute-start.47 = (f32[1,512,128]{2,1,0:T(8,128)S(1)}, f32[1,512,128]{2,1,0:T(8,128)S(1)}, u32[]{:S(2)}, u32[]{:S(2)}) collective-permute-start(f32[1,512,128]{2,1,0:T(8,128)S(1)} %get-tuple-element.103), channel_id=1, source_target_pairs={{0,1},{1,2},{2,3},{4,5},{5,6},{6,7},{8,9},{9,10},{10,11},{12,13},{... | collective-permute-start | bytes 786440 | tf_op jit(solution)/shard_map/ppermute | solution.py:21
  324.0 7.2 %collective-permute-start.49 = (f32[1,512,128]{2,1,0:T(8,128)S(1)}, f32[1,512,128]{2,1,0:T(8,128)S(1)}, u32[]{:S(2)}, u32[]{:S(2)}) collective-permute-start(f32[1,512,128]{2,1,0:T(8,128)S(1)} %get-tuple-element.101), channel_id=1, source_target_pairs={{0,1},{1,2},{2,3},{4,5},{5,6},{6,7},{8,9},{9,10},{10,11},{12,13},{... | collective-permute-start | bytes 786440 | tf_op jit(solution)/shard_map/ppermute | solution.py:21
  334.8 7.2 %collective-permute-start.51 = (f32[1,512,128]{2,1,0:T(8,128)S(1)}, f32[1,512,128]{2,1,0:T(8,128)S(1)}, u32[]{:S(2)}, u32[]{:S(2)}) collective-permute-start(f32[1,512,128]{2,1,0:T(8,128)S(1)} %get-tuple-element.99), channel_id=1, source_target_pairs={{0,1},{1,2},{2,3},{4,5},{5,6},{6,7},{8,9},{9,10},{10,11},{12,13},{... | collective-permute-start | bytes 786440 | tf_op jit(solution)/shard_map/ppermute | solution.py:21
  345.6 7.2 %collective-permute-start.53 = (f32[1,512,128]{2,1,0:T(8,128)S(1)}, f32[1,512,128]{2,1,0:T(8,128)S(1)}, u32[]{:S(2)}, u32[]{:S(2)}) collective-permute-start(f32[1,512,128]{2,1,0:T(8,128)S(1)} %get-tuple-element.97), channel_id=1, source_target_pairs={{0,1},{1,2},{2,3},{4,5},{5,6},{6,7},{8,9},{9,10},{10,11},{12,13},{... | collective-permute-start | bytes 786440 | tf_op jit(solution)/shard_map/ppermute | solution.py:21
  356.4 7.2 %collective-permute-start.55 = (f32[1,512,128]{2,1,0:T(8,128)S(1)}, f32[1,512,128]{2,1,0:T(8,128)S(1)}, u32[]{:S(2)}, u32[]{:S(2)}) collective-permute-start(f32[1,512,128]{2,1,0:T(8,128)S(1)} %get-tuple-element.95), channel_id=1, source_target_pairs={{0,1},{1,2},{2,3},{4,5},{5,6},{6,7},{8,9},{9,10},{10,11},{12,13},{... | collective-permute-start | bytes 786440 | tf_op jit(solution)/shard_map/ppermute | solution.py:21
  367.2 7.2 %collective-permute-start.57 = (f32[1,512,128]{2,1,0:T(8,128)S(1)}, f32[1,512,128]{2,1,0:T(8,128)S(1)}, u32[]{:S(2)}, u32[]{:S(2)}) collective-permute-start(f32[1,512,128]{2,1,0:T(8,128)S(1)} %get-tuple-element.93), channel_id=1, source_target_pairs={{0,1},{1,2},{2,3},{4,5},{5,6},{6,7},{8,9},{9,10},{10,11},{12,13},{... | collective-permute-start | bytes 786440 | tf_op jit(solution)/shard_map/ppermute | solution.py:21
  376.7 1.3 collective-permute-start.58
  378.0 7.4 %collective-permute-start.59 = (f32[1,512,128]{2,1,0:T(8,128)S(1)}, f32[1,512,128]{2,1,0:T(8,128)S(1)}, u32[]{:S(2)}, u32[]{:S(2)}) collective-permute-start(f32[1,512,128]{2,1,0:T(8,128)S(1)} %get-tuple-element.91), channel_id=1, source_target_pairs={{0,1},{1,2},{2,3},{4,5},{5,6},{6,7},{8,9},{9,10},{10,11},{12,13},{... | collective-permute-start | bytes 786440 | tf_op jit(solution)/shard_map/ppermute | solution.py:21
  389.1 7.2 %collective-permute-start.61 = (f32[1,512,128]{2,1,0:T(8,128)S(1)}, f32[1,512,128]{2,1,0:T(8,128)S(1)}, u32[]{:S(2)}, u32[]{:S(2)}) collective-permute-start(f32[1,512,128]{2,1,0:T(8,128)S(1)} %get-tuple-element.89), channel_id=1, source_target_pairs={{0,1},{1,2},{2,3},{4,5},{5,6},{6,7},{8,9},{9,10},{10,11},{12,13},{... | collective-permute-start | bytes 786440 | tf_op jit(solution)/shard_map/ppermute | solution.py:21
  398.6 1.3 collective-permute-start.62
  399.9 7.2 %collective-permute-start.63 = (f32[1,512,128]{2,1,0:T(8,128)S(1)}, f32[1,512,128]{2,1,0:T(8,128)S(1)}, u32[]{:S(2)}, u32[]{:S(2)}) collective-permute-start(f32[1,512,128]{2,1,0:T(8,128)S(1)} %get-tuple-element.87), channel_id=1, source_target_pairs={{0,1},{1,2},{2,3},{4,5},{5,6},{6,7},{8,9},{9,10},{10,11},{12,13},{... | collective-permute-start | bytes 786440 | tf_op jit(solution)/shard_map/ppermute | solution.py:21
  409.4 1.3 collective-permute-start.64
  410.7 7.2 %collective-permute-start.65 = (f32[1,512,128]{2,1,0:T(8,128)S(1)}, f32[1,512,128]{2,1,0:T(8,128)S(1)}, u32[]{:S(2)}, u32[]{:S(2)}) collective-permute-start(f32[1,512,128]{2,1,0:T(8,128)S(1)} %get-tuple-element.85), channel_id=1, source_target_pairs={{0,1},{1,2},{2,3},{4,5},{5,6},{6,7},{8,9},{9,10},{10,11},{12,13},{... | collective-permute-start | bytes 786440 | tf_op jit(solution)/shard_map/ppermute | solution.py:21
  421.5 7.2 %collective-permute-start.67 = (f32[1,512,128]{2,1,0:T(8,128)S(1)}, f32[1,512,128]{2,1,0:T(8,128)S(1)}, u32[]{:S(2)}, u32[]{:S(2)}) collective-permute-start(f32[1,512,128]{2,1,0:T(8,128)S(1)} %get-tuple-element.83), channel_id=1, source_target_pairs={{0,1},{1,2},{2,3},{4,5},{5,6},{6,7},{8,9},{9,10},{10,11},{12,13},{... | collective-permute-start | bytes 786440 | tf_op jit(solution)/shard_map/ppermute | solution.py:21
  432.3 7.2 %collective-permute-start.69 = (f32[1,512,128]{2,1,0:T(8,128)S(1)}, f32[1,512,128]{2,1,0:T(8,128)S(1)}, u32[]{:S(2)}, u32[]{:S(2)}) collective-permute-start(f32[1,512,128]{2,1,0:T(8,128)S(1)} %get-tuple-element.81), channel_id=1, source_target_pairs={{0,1},{1,2},{2,3},{4,5},{5,6},{6,7},{8,9},{9,10},{10,11},{12,13},{... | collective-permute-start | bytes 786440 | tf_op jit(solution)/shard_map/ppermute | solution.py:21
  443.1 7.2 %collective-permute-start.71 = (f32[1,512,128]{2,1,0:T(8,128)S(1)}, f32[1,512,128]{2,1,0:T(8,128)S(1)}, u32[]{:S(2)}, u32[]{:S(2)}) collective-permute-start(f32[1,512,128]{2,1,0:T(8,128)S(1)} %get-tuple-element.79), channel_id=1, source_target_pairs={{0,1},{1,2},{2,3},{4,5},{5,6},{6,7},{8,9},{9,10},{10,11},{12,13},{... | collective-permute-start | bytes 786440 | tf_op jit(solution)/shard_map/ppermute | solution.py:21
  453.1 2.4 fusion.8
  456.7 104.8 %all-reduce.39.cloned.1.call-done = f32[32,16384]{1,0:T(8,128)} async-done(((f32[32,16384]{1,0:T(8,128)}), f32[32,16384]{1,0:T(8,128)}) %all-reduce.39.cloned.1.call-update) | async-done | bytes 2097168
  (217 shorter events, 103.5 us)
Async XLA Ops:
  7.2 55.0 %all-gather.2.cloned.1.call-start = ((), (), s32[]{:S(2)}) async-start(), calls=%async_computation | async-start | bytes 2359296 | tf_op jit(solution)/shard_map/all_gather | solution.py:75
  7.9 553.6 %all-reduce.39.cloned.1.call-start = ((), (), s32[]{:S(2)}) async-start(), calls=%async_computation.1 | async-start | bytes 4194304
  83.7 8.5 %collective-permute-start.4 = (f32[1,512,128]{2,1,0:T(8,128)S(1)}, f32[1,512,128]{2,1,0:T(8,128)S(1)}, u32[]{:S(2)}, u32[]{:S(2)}) collective-permute-start(f32[1,512,128]{2,1,0:T(8,128)S(1)} %get-tuple-element.146), channel_id=1, source_target_pairs={{1,0},{2,1},{3,2},{5,4},{6,5},{7,6},{9,8},{10,9},{11,10},{13,12},{... | collective-permute-start | bytes 786440 | tf_op jit(solution)/shard_map/ppermute | solution.py:22
  85.0 8.3 %collective-permute-start.5 = (f32[1,512,128]{2,1,0:T(8,128)S(1)}, f32[1,512,128]{2,1,0:T(8,128)S(1)}, u32[]{:S(2)}, u32[]{:S(2)}) collective-permute-start(f32[1,512,128]{2,1,0:T(8,128)S(1)} %get-tuple-element.145), channel_id=1, source_target_pairs={{0,1},{1,2},{2,3},{4,5},{5,6},{6,7},{8,9},{9,10},{10,11},{12,13},{... | collective-permute-start | bytes 786440 | tf_op jit(solution)/shard_map/ppermute | solution.py:21
  94.6 8.5 %collective-permute-start.6 = (f32[1,512,128]{2,1,0:T(8,128)S(1)}, f32[1,512,128]{2,1,0:T(8,128)S(1)}, u32[]{:S(2)}, u32[]{:S(2)}) collective-permute-start(f32[1,512,128]{2,1,0:T(8,128)S(1)} %get-tuple-element.144), channel_id=1, source_target_pairs={{1,0},{2,1},{3,2},{5,4},{6,5},{7,6},{9,8},{10,9},{11,10},{13,12},{... | collective-permute-start | bytes 786440 | tf_op jit(solution)/shard_map/ppermute | solution.py:22
  95.9 8.3 %collective-permute-start.7 = (f32[1,512,128]{2,1,0:T(8,128)S(1)}, f32[1,512,128]{2,1,0:T(8,128)S(1)}, u32[]{:S(2)}, u32[]{:S(2)}) collective-permute-start(f32[1,512,128]{2,1,0:T(8,128)S(1)} %get-tuple-element.143), channel_id=1, source_target_pairs={{0,1},{1,2},{2,3},{4,5},{5,6},{6,7},{8,9},{9,10},{10,11},{12,13},{... | collective-permute-start | bytes 786440 | tf_op jit(solution)/shard_map/ppermute | solution.py:21
  105.4 8.5 %collective-permute-start.8 = (f32[1,512,128]{2,1,0:T(8,128)S(1)}, f32[1,512,128]{2,1,0:T(8,128)S(1)}, u32[]{:S(2)}, u32[]{:S(2)}) collective-permute-start(f32[1,512,128]{2,1,0:T(8,128)S(1)} %get-tuple-element.142), channel_id=1, source_target_pairs={{1,0},{2,1},{3,2},{5,4},{6,5},{7,6},{9,8},{10,9},{11,10},{13,12},{... | collective-permute-start | bytes 786440 | tf_op jit(solution)/shard_map/ppermute | solution.py:22
  106.7 8.3 %collective-permute-start.9 = (f32[1,512,128]{2,1,0:T(8,128)S(1)}, f32[1,512,128]{2,1,0:T(8,128)S(1)}, u32[]{:S(2)}, u32[]{:S(2)}) collective-permute-start(f32[1,512,128]{2,1,0:T(8,128)S(1)} %get-tuple-element.141), channel_id=1, source_target_pairs={{0,1},{1,2},{2,3},{4,5},{5,6},{6,7},{8,9},{9,10},{10,11},{12,13},{... | collective-permute-start | bytes 786440 | tf_op jit(solution)/shard_map/ppermute | solution.py:21
  116.2 9.0 %collective-permute-start.10 = (f32[1,512,128]{2,1,0:T(8,128)S(1)}, f32[1,512,128]{2,1,0:T(8,128)S(1)}, u32[]{:S(2)}, u32[]{:S(2)}) collective-permute-start(f32[1,512,128]{2,1,0:T(8,128)S(1)} %get-tuple-element.140), channel_id=1, source_target_pairs={{1,0},{2,1},{3,2},{5,4},{6,5},{7,6},{9,8},{10,9},{11,10},{13,12},{... | collective-permute-start | bytes 786440 | tf_op jit(solution)/shard_map/ppermute | solution.py:22
  117.5 8.3 %collective-permute-start.11 = (f32[1,512,128]{2,1,0:T(8,128)S(1)}, f32[1,512,128]{2,1,0:T(8,128)S(1)}, u32[]{:S(2)}, u32[]{:S(2)}) collective-permute-start(f32[1,512,128]{2,1,0:T(8,128)S(1)} %get-tuple-element.139), channel_id=1, source_target_pairs={{0,1},{1,2},{2,3},{4,5},{5,6},{6,7},{8,9},{9,10},{10,11},{12,13},{... | collective-permute-start | bytes 786440 | tf_op jit(solution)/shard_map/ppermute | solution.py:21
  127.2 8.5 %collective-permute-start.12 = (f32[1,512,128]{2,1,0:T(8,128)S(1)}, f32[1,512,128]{2,1,0:T(8,128)S(1)}, u32[]{:S(2)}, u32[]{:S(2)}) collective-permute-start(f32[1,512,128]{2,1,0:T(8,128)S(1)} %get-tuple-element.138), channel_id=1, source_target_pairs={{1,0},{2,1},{3,2},{5,4},{6,5},{7,6},{9,8},{10,9},{11,10},{13,12},{... | collective-permute-start | bytes 786440 | tf_op jit(solution)/shard_map/ppermute | solution.py:22
  128.5 8.3 %collective-permute-start.13 = (f32[1,512,128]{2,1,0:T(8,128)S(1)}, f32[1,512,128]{2,1,0:T(8,128)S(1)}, u32[]{:S(2)}, u32[]{:S(2)}) collective-permute-start(f32[1,512,128]{2,1,0:T(8,128)S(1)} %get-tuple-element.137), channel_id=1, source_target_pairs={{0,1},{1,2},{2,3},{4,5},{5,6},{6,7},{8,9},{9,10},{10,11},{12,13},{... | collective-permute-start | bytes 786440 | tf_op jit(solution)/shard_map/ppermute | solution.py:21
  138.0 8.5 %collective-permute-start.14 = (f32[1,512,128]{2,1,0:T(8,128)S(1)}, f32[1,512,128]{2,1,0:T(8,128)S(1)}, u32[]{:S(2)}, u32[]{:S(2)}) collective-permute-start(f32[1,512,128]{2,1,0:T(8,128)S(1)} %get-tuple-element.136), channel_id=1, source_target_pairs={{1,0},{2,1},{3,2},{5,4},{6,5},{7,6},{9,8},{10,9},{11,10},{13,12},{... | collective-permute-start | bytes 786440 | tf_op jit(solution)/shard_map/ppermute | solution.py:22
  139.3 8.3 %collective-permute-start.15 = (f32[1,512,128]{2,1,0:T(8,128)S(1)}, f32[1,512,128]{2,1,0:T(8,128)S(1)}, u32[]{:S(2)}, u32[]{:S(2)}) collective-permute-start(f32[1,512,128]{2,1,0:T(8,128)S(1)} %get-tuple-element.135), channel_id=1, source_target_pairs={{0,1},{1,2},{2,3},{4,5},{5,6},{6,7},{8,9},{9,10},{10,11},{12,13},{... | collective-permute-start | bytes 786440 | tf_op jit(solution)/shard_map/ppermute | solution.py:21
  148.8 8.5 %collective-permute-start.16 = (f32[1,512,128]{2,1,0:T(8,128)S(1)}, f32[1,512,128]{2,1,0:T(8,128)S(1)}, u32[]{:S(2)}, u32[]{:S(2)}) collective-permute-start(f32[1,512,128]{2,1,0:T(8,128)S(1)} %get-tuple-element.134), channel_id=1, source_target_pairs={{1,0},{2,1},{3,2},{5,4},{6,5},{7,6},{9,8},{10,9},{11,10},{13,12},{... | collective-permute-start | bytes 786440 | tf_op jit(solution)/shard_map/ppermute | solution.py:22
  150.1 8.3 %collective-permute-start.17 = (f32[1,512,128]{2,1,0:T(8,128)S(1)}, f32[1,512,128]{2,1,0:T(8,128)S(1)}, u32[]{:S(2)}, u32[]{:S(2)}) collective-permute-start(f32[1,512,128]{2,1,0:T(8,128)S(1)} %get-tuple-element.133), channel_id=1, source_target_pairs={{0,1},{1,2},{2,3},{4,5},{5,6},{6,7},{8,9},{9,10},{10,11},{12,13},{... | collective-permute-start | bytes 786440 | tf_op jit(solution)/shard_map/ppermute | solution.py:21
  159.6 8.5 %collective-permute-start.18 = (f32[1,512,128]{2,1,0:T(8,128)S(1)}, f32[1,512,128]{2,1,0:T(8,128)S(1)}, u32[]{:S(2)}, u32[]{:S(2)}) collective-permute-start(f32[1,512,128]{2,1,0:T(8,128)S(1)} %get-tuple-element.132), channel_id=1, source_target_pairs={{1,0},{2,1},{3,2},{5,4},{6,5},{7,6},{9,8},{10,9},{11,10},{13,12},{... | collective-permute-start | bytes 786440 | tf_op jit(solution)/shard_map/ppermute | solution.py:22
  160.9 8.3 %collective-permute-start.19 = (f32[1,512,128]{2,1,0:T(8,128)S(1)}, f32[1,512,128]{2,1,0:T(8,128)S(1)}, u32[]{:S(2)}, u32[]{:S(2)}) collective-permute-start(f32[1,512,128]{2,1,0:T(8,128)S(1)} %get-tuple-element.131), channel_id=1, source_target_pairs={{0,1},{1,2},{2,3},{4,5},{5,6},{6,7},{8,9},{9,10},{10,11},{12,13},{... | collective-permute-start | bytes 786440 | tf_op jit(solution)/shard_map/ppermute | solution.py:21
  170.5 8.5 %collective-permute-start.20 = (f32[1,512,128]{2,1,0:T(8,128)S(1)}, f32[1,512,128]{2,1,0:T(8,128)S(1)}, u32[]{:S(2)}, u32[]{:S(2)}) collective-permute-start(f32[1,512,128]{2,1,0:T(8,128)S(1)} %get-tuple-element.130), channel_id=1, source_target_pairs={{1,0},{2,1},{3,2},{5,4},{6,5},{7,6},{9,8},{10,9},{11,10},{13,12},{... | collective-permute-start | bytes 786440 | tf_op jit(solution)/shard_map/ppermute | solution.py:22
  171.8 8.3 %collective-permute-start.21 = (f32[1,512,128]{2,1,0:T(8,128)S(1)}, f32[1,512,128]{2,1,0:T(8,128)S(1)}, u32[]{:S(2)}, u32[]{:S(2)}) collective-permute-start(f32[1,512,128]{2,1,0:T(8,128)S(1)} %get-tuple-element.129), channel_id=1, source_target_pairs={{0,1},{1,2},{2,3},{4,5},{5,6},{6,7},{8,9},{9,10},{10,11},{12,13},{... | collective-permute-start | bytes 786440 | tf_op jit(solution)/shard_map/ppermute | solution.py:21
  181.3 8.5 %collective-permute-start.22 = (f32[1,512,128]{2,1,0:T(8,128)S(1)}, f32[1,512,128]{2,1,0:T(8,128)S(1)}, u32[]{:S(2)}, u32[]{:S(2)}) collective-permute-start(f32[1,512,128]{2,1,0:T(8,128)S(1)} %get-tuple-element.128), channel_id=1, source_target_pairs={{1,0},{2,1},{3,2},{5,4},{6,5},{7,6},{9,8},{10,9},{11,10},{13,12},{... | collective-permute-start | bytes 786440 | tf_op jit(solution)/shard_map/ppermute | solution.py:22
  182.6 8.3 %collective-permute-start.23 = (f32[1,512,128]{2,1,0:T(8,128)S(1)}, f32[1,512,128]{2,1,0:T(8,128)S(1)}, u32[]{:S(2)}, u32[]{:S(2)}) collective-permute-start(f32[1,512,128]{2,1,0:T(8,128)S(1)} %get-tuple-element.127), channel_id=1, source_target_pairs={{0,1},{1,2},{2,3},{4,5},{5,6},{6,7},{8,9},{9,10},{10,11},{12,13},{... | collective-permute-start | bytes 786440 | tf_op jit(solution)/shard_map/ppermute | solution.py:21
  192.3 8.5 %collective-permute-start.24 = (f32[1,512,128]{2,1,0:T(8,128)S(1)}, f32[1,512,128]{2,1,0:T(8,128)S(1)}, u32[]{:S(2)}, u32[]{:S(2)}) collective-permute-start(f32[1,512,128]{2,1,0:T(8,128)S(1)} %get-tuple-element.126), channel_id=1, source_target_pairs={{1,0},{2,1},{3,2},{5,4},{6,5},{7,6},{9,8},{10,9},{11,10},{13,12},{... | collective-permute-start | bytes 786440 | tf_op jit(solution)/shard_map/ppermute | solution.py:22
  193.6 8.3 %collective-permute-start.25 = (f32[1,512,128]{2,1,0:T(8,128)S(1)}, f32[1,512,128]{2,1,0:T(8,128)S(1)}, u32[]{:S(2)}, u32[]{:S(2)}) collective-permute-start(f32[1,512,128]{2,1,0:T(8,128)S(1)} %get-tuple-element.125), channel_id=1, source_target_pairs={{0,1},{1,2},{2,3},{4,5},{5,6},{6,7},{8,9},{9,10},{10,11},{12,13},{... | collective-permute-start | bytes 786440 | tf_op jit(solution)/shard_map/ppermute | solution.py:21
  203.1 8.7 %collective-permute-start.26 = (f32[1,512,128]{2,1,0:T(8,128)S(1)}, f32[1,512,128]{2,1,0:T(8,128)S(1)}, u32[]{:S(2)}, u32[]{:S(2)}) collective-permute-start(f32[1,512,128]{2,1,0:T(8,128)S(1)} %get-tuple-element.124), channel_id=1, source_target_pairs={{1,0},{2,1},{3,2},{5,4},{6,5},{7,6},{9,8},{10,9},{11,10},{13,12},{... | collective-permute-start | bytes 786440 | tf_op jit(solution)/shard_map/ppermute | solution.py:22
  204.4 8.3 %collective-permute-start.27 = (f32[1,512,128]{2,1,0:T(8,128)S(1)}, f32[1,512,128]{2,1,0:T(8,128)S(1)}, u32[]{:S(2)}, u32[]{:S(2)}) collective-permute-start(f32[1,512,128]{2,1,0:T(8,128)S(1)} %get-tuple-element.123), channel_id=1, source_target_pairs={{0,1},{1,2},{2,3},{4,5},{5,6},{6,7},{8,9},{9,10},{10,11},{12,13},{... | collective-permute-start | bytes 786440 | tf_op jit(solution)/shard_map/ppermute | solution.py:21
  213.9 8.5 %collective-permute-start.28 = (f32[1,512,128]{2,1,0:T(8,128)S(1)}, f32[1,512,128]{2,1,0:T(8,128)S(1)}, u32[]{:S(2)}, u32[]{:S(2)}) collective-permute-start(f32[1,512,128]{2,1,0:T(8,128)S(1)} %get-tuple-element.122), channel_id=1, source_target_pairs={{1,0},{2,1},{3,2},{5,4},{6,5},{7,6},{9,8},{10,9},{11,10},{13,12},{... | collective-permute-start | bytes 786440 | tf_op jit(solution)/shard_map/ppermute | solution.py:22
  215.2 8.3 %collective-permute-start.29 = (f32[1,512,128]{2,1,0:T(8,128)S(1)}, f32[1,512,128]{2,1,0:T(8,128)S(1)}, u32[]{:S(2)}, u32[]{:S(2)}) collective-permute-start(f32[1,512,128]{2,1,0:T(8,128)S(1)} %get-tuple-element.121), channel_id=1, source_target_pairs={{0,1},{1,2},{2,3},{4,5},{5,6},{6,7},{8,9},{9,10},{10,11},{12,13},{... | collective-permute-start | bytes 786440 | tf_op jit(solution)/shard_map/ppermute | solution.py:21
  224.8 8.5 %collective-permute-start.30 = (f32[1,512,128]{2,1,0:T(8,128)S(1)}, f32[1,512,128]{2,1,0:T(8,128)S(1)}, u32[]{:S(2)}, u32[]{:S(2)}) collective-permute-start(f32[1,512,128]{2,1,0:T(8,128)S(1)} %get-tuple-element.120), channel_id=1, source_target_pairs={{1,0},{2,1},{3,2},{5,4},{6,5},{7,6},{9,8},{10,9},{11,10},{13,12},{... | collective-permute-start | bytes 786440 | tf_op jit(solution)/shard_map/ppermute | solution.py:22
  226.1 8.3 %collective-permute-start.31 = (f32[1,512,128]{2,1,0:T(8,128)S(1)}, f32[1,512,128]{2,1,0:T(8,128)S(1)}, u32[]{:S(2)}, u32[]{:S(2)}) collective-permute-start(f32[1,512,128]{2,1,0:T(8,128)S(1)} %get-tuple-element.119), channel_id=1, source_target_pairs={{0,1},{1,2},{2,3},{4,5},{5,6},{6,7},{8,9},{9,10},{10,11},{12,13},{... | collective-permute-start | bytes 786440 | tf_op jit(solution)/shard_map/ppermute | solution.py:21
  235.6 8.5 %collective-permute-start.32 = (f32[1,512,128]{2,1,0:T(8,128)S(1)}, f32[1,512,128]{2,1,0:T(8,128)S(1)}, u32[]{:S(2)}, u32[]{:S(2)}) collective-permute-start(f32[1,512,128]{2,1,0:T(8,128)S(1)} %get-tuple-element.118), channel_id=1, source_target_pairs={{1,0},{2,1},{3,2},{5,4},{6,5},{7,6},{9,8},{10,9},{11,10},{13,12},{... | collective-permute-start | bytes 786440 | tf_op jit(solution)/shard_map/ppermute | solution.py:22
  236.9 8.3 %collective-permute-start.33 = (f32[1,512,128]{2,1,0:T(8,128)S(1)}, f32[1,512,128]{2,1,0:T(8,128)S(1)}, u32[]{:S(2)}, u32[]{:S(2)}) collective-permute-start(f32[1,512,128]{2,1,0:T(8,128)S(1)} %get-tuple-element.117), channel_id=1, source_target_pairs={{0,1},{1,2},{2,3},{4,5},{5,6},{6,7},{8,9},{9,10},{10,11},{12,13},{... | collective-permute-start | bytes 786440 | tf_op jit(solution)/shard_map/ppermute | solution.py:21
  246.4 8.6 %collective-permute-start.34 = (f32[1,512,128]{2,1,0:T(8,128)S(1)}, f32[1,512,128]{2,1,0:T(8,128)S(1)}, u32[]{:S(2)}, u32[]{:S(2)}) collective-permute-start(f32[1,512,128]{2,1,0:T(8,128)S(1)} %get-tuple-element.116), channel_id=1, source_target_pairs={{1,0},{2,1},{3,2},{5,4},{6,5},{7,6},{9,8},{10,9},{11,10},{13,12},{... | collective-permute-start | bytes 786440 | tf_op jit(solution)/shard_map/ppermute | solution.py:22
  247.8 8.3 %collective-permute-start.35 = (f32[1,512,128]{2,1,0:T(8,128)S(1)}, f32[1,512,128]{2,1,0:T(8,128)S(1)}, u32[]{:S(2)}, u32[]{:S(2)}) collective-permute-start(f32[1,512,128]{2,1,0:T(8,128)S(1)} %get-tuple-element.115), channel_id=1, source_target_pairs={{0,1},{1,2},{2,3},{4,5},{5,6},{6,7},{8,9},{9,10},{10,11},{12,13},{... | collective-permute-start | bytes 786440 | tf_op jit(solution)/shard_map/ppermute | solution.py:21
  257.5 8.5 %collective-permute-start.36 = (f32[1,512,128]{2,1,0:T(8,128)S(1)}, f32[1,512,128]{2,1,0:T(8,128)S(1)}, u32[]{:S(2)}, u32[]{:S(2)}) collective-permute-start(f32[1,512,128]{2,1,0:T(8,128)S(1)} %get-tuple-element.114), channel_id=1, source_target_pairs={{1,0},{2,1},{3,2},{5,4},{6,5},{7,6},{9,8},{10,9},{11,10},{13,12},{... | collective-permute-start | bytes 786440 | tf_op jit(solution)/shard_map/ppermute | solution.py:22
  258.8 8.3 %collective-permute-start.37 = (f32[1,512,128]{2,1,0:T(8,128)S(1)}, f32[1,512,128]{2,1,0:T(8,128)S(1)}, u32[]{:S(2)}, u32[]{:S(2)}) collective-permute-start(f32[1,512,128]{2,1,0:T(8,128)S(1)} %get-tuple-element.113), channel_id=1, source_target_pairs={{0,1},{1,2},{2,3},{4,5},{5,6},{6,7},{8,9},{9,10},{10,11},{12,13},{... | collective-permute-start | bytes 786440 | tf_op jit(solution)/shard_map/ppermute | solution.py:21
  268.4 8.5 %collective-permute-start.38 = (f32[1,512,128]{2,1,0:T(8,128)S(1)}, f32[1,512,128]{2,1,0:T(8,128)S(1)}, u32[]{:S(2)}, u32[]{:S(2)}) collective-permute-start(f32[1,512,128]{2,1,0:T(8,128)S(1)} %get-tuple-element.112), channel_id=1, source_target_pairs={{1,0},{2,1},{3,2},{5,4},{6,5},{7,6},{9,8},{10,9},{11,10},{13,12},{... | collective-permute-start | bytes 786440 | tf_op jit(solution)/shard_map/ppermute | solution.py:22
  269.7 8.3 %collective-permute-start.39 = (f32[1,512,128]{2,1,0:T(8,128)S(1)}, f32[1,512,128]{2,1,0:T(8,128)S(1)}, u32[]{:S(2)}, u32[]{:S(2)}) collective-permute-start(f32[1,512,128]{2,1,0:T(8,128)S(1)} %get-tuple-element.111), channel_id=1, source_target_pairs={{0,1},{1,2},{2,3},{4,5},{5,6},{6,7},{8,9},{9,10},{10,11},{12,13},{... | collective-permute-start | bytes 786440 | tf_op jit(solution)/shard_map/ppermute | solution.py:21
  279.2 8.5 %collective-permute-start.40 = (f32[1,512,128]{2,1,0:T(8,128)S(1)}, f32[1,512,128]{2,1,0:T(8,128)S(1)}, u32[]{:S(2)}, u32[]{:S(2)}) collective-permute-start(f32[1,512,128]{2,1,0:T(8,128)S(1)} %get-tuple-element.110), channel_id=1, source_target_pairs={{1,0},{2,1},{3,2},{5,4},{6,5},{7,6},{9,8},{10,9},{11,10},{13,12},{... | collective-permute-start | bytes 786440 | tf_op jit(solution)/shard_map/ppermute | solution.py:22
  280.5 8.3 %collective-permute-start.41 = (f32[1,512,128]{2,1,0:T(8,128)S(1)}, f32[1,512,128]{2,1,0:T(8,128)S(1)}, u32[]{:S(2)}, u32[]{:S(2)}) collective-permute-start(f32[1,512,128]{2,1,0:T(8,128)S(1)} %get-tuple-element.109), channel_id=1, source_target_pairs={{0,1},{1,2},{2,3},{4,5},{5,6},{6,7},{8,9},{9,10},{10,11},{12,13},{... | collective-permute-start | bytes 786440 | tf_op jit(solution)/shard_map/ppermute | solution.py:21
  290.0 8.7 %collective-permute-start.42 = (f32[1,512,128]{2,1,0:T(8,128)S(1)}, f32[1,512,128]{2,1,0:T(8,128)S(1)}, u32[]{:S(2)}, u32[]{:S(2)}) collective-permute-start(f32[1,512,128]{2,1,0:T(8,128)S(1)} %get-tuple-element.108), channel_id=1, source_target_pairs={{1,0},{2,1},{3,2},{5,4},{6,5},{7,6},{9,8},{10,9},{11,10},{13,12},{... | collective-permute-start | bytes 786440 | tf_op jit(solution)/shard_map/ppermute | solution.py:22
  291.3 8.3 %collective-permute-start.43 = (f32[1,512,128]{2,1,0:T(8,128)S(1)}, f32[1,512,128]{2,1,0:T(8,128)S(1)}, u32[]{:S(2)}, u32[]{:S(2)}) collective-permute-start(f32[1,512,128]{2,1,0:T(8,128)S(1)} %get-tuple-element.107), channel_id=1, source_target_pairs={{0,1},{1,2},{2,3},{4,5},{5,6},{6,7},{8,9},{9,10},{10,11},{12,13},{... | collective-permute-start | bytes 786440 | tf_op jit(solution)/shard_map/ppermute | solution.py:21
  300.8 8.5 %collective-permute-start.44 = (f32[1,512,128]{2,1,0:T(8,128)S(1)}, f32[1,512,128]{2,1,0:T(8,128)S(1)}, u32[]{:S(2)}, u32[]{:S(2)}) collective-permute-start(f32[1,512,128]{2,1,0:T(8,128)S(1)} %get-tuple-element.106), channel_id=1, source_target_pairs={{1,0},{2,1},{3,2},{5,4},{6,5},{7,6},{9,8},{10,9},{11,10},{13,12},{... | collective-permute-start | bytes 786440 | tf_op jit(solution)/shard_map/ppermute | solution.py:22
  302.1 8.3 %collective-permute-start.45 = (f32[1,512,128]{2,1,0:T(8,128)S(1)}, f32[1,512,128]{2,1,0:T(8,128)S(1)}, u32[]{:S(2)}, u32[]{:S(2)}) collective-permute-start(f32[1,512,128]{2,1,0:T(8,128)S(1)} %get-tuple-element.105), channel_id=1, source_target_pairs={{0,1},{1,2},{2,3},{4,5},{5,6},{6,7},{8,9},{9,10},{10,11},{12,13},{... | collective-permute-start | bytes 786440 | tf_op jit(solution)/shard_map/ppermute | solution.py:21
  311.6 8.5 %collective-permute-start.46 = (f32[1,512,128]{2,1,0:T(8,128)S(1)}, f32[1,512,128]{2,1,0:T(8,128)S(1)}, u32[]{:S(2)}, u32[]{:S(2)}) collective-permute-start(f32[1,512,128]{2,1,0:T(8,128)S(1)} %get-tuple-element.104), channel_id=1, source_target_pairs={{1,0},{2,1},{3,2},{5,4},{6,5},{7,6},{9,8},{10,9},{11,10},{13,12},{... | collective-permute-start | bytes 786440 | tf_op jit(solution)/shard_map/ppermute | solution.py:22
  312.9 8.3 %collective-permute-start.47 = (f32[1,512,128]{2,1,0:T(8,128)S(1)}, f32[1,512,128]{2,1,0:T(8,128)S(1)}, u32[]{:S(2)}, u32[]{:S(2)}) collective-permute-start(f32[1,512,128]{2,1,0:T(8,128)S(1)} %get-tuple-element.103), channel_id=1, source_target_pairs={{0,1},{1,2},{2,3},{4,5},{5,6},{6,7},{8,9},{9,10},{10,11},{12,13},{... | collective-permute-start | bytes 786440 | tf_op jit(solution)/shard_map/ppermute | solution.py:21
  322.7 8.5 %collective-permute-start.48 = (f32[1,512,128]{2,1,0:T(8,128)S(1)}, f32[1,512,128]{2,1,0:T(8,128)S(1)}, u32[]{:S(2)}, u32[]{:S(2)}) collective-permute-start(f32[1,512,128]{2,1,0:T(8,128)S(1)} %get-tuple-element.102), channel_id=1, source_target_pairs={{1,0},{2,1},{3,2},{5,4},{6,5},{7,6},{9,8},{10,9},{11,10},{13,12},{... | collective-permute-start | bytes 786440 | tf_op jit(solution)/shard_map/ppermute | solution.py:22
  324.0 8.3 %collective-permute-start.49 = (f32[1,512,128]{2,1,0:T(8,128)S(1)}, f32[1,512,128]{2,1,0:T(8,128)S(1)}, u32[]{:S(2)}, u32[]{:S(2)}) collective-permute-start(f32[1,512,128]{2,1,0:T(8,128)S(1)} %get-tuple-element.101), channel_id=1, source_target_pairs={{0,1},{1,2},{2,3},{4,5},{5,6},{6,7},{8,9},{9,10},{10,11},{12,13},{... | collective-permute-start | bytes 786440 | tf_op jit(solution)/shard_map/ppermute | solution.py:21
  333.5 8.5 %collective-permute-start.50 = (f32[1,512,128]{2,1,0:T(8,128)S(1)}, f32[1,512,128]{2,1,0:T(8,128)S(1)}, u32[]{:S(2)}, u32[]{:S(2)}) collective-permute-start(f32[1,512,128]{2,1,0:T(8,128)S(1)} %get-tuple-element.100), channel_id=1, source_target_pairs={{1,0},{2,1},{3,2},{5,4},{6,5},{7,6},{9,8},{10,9},{11,10},{13,12},{... | collective-permute-start | bytes 786440 | tf_op jit(solution)/shard_map/ppermute | solution.py:22
  334.8 8.3 %collective-permute-start.51 = (f32[1,512,128]{2,1,0:T(8,128)S(1)}, f32[1,512,128]{2,1,0:T(8,128)S(1)}, u32[]{:S(2)}, u32[]{:S(2)}) collective-permute-start(f32[1,512,128]{2,1,0:T(8,128)S(1)} %get-tuple-element.99), channel_id=1, source_target_pairs={{0,1},{1,2},{2,3},{4,5},{5,6},{6,7},{8,9},{9,10},{10,11},{12,13},{... | collective-permute-start | bytes 786440 | tf_op jit(solution)/shard_map/ppermute | solution.py:21
  344.3 8.5 %collective-permute-start.52 = (f32[1,512,128]{2,1,0:T(8,128)S(1)}, f32[1,512,128]{2,1,0:T(8,128)S(1)}, u32[]{:S(2)}, u32[]{:S(2)}) collective-permute-start(f32[1,512,128]{2,1,0:T(8,128)S(1)} %get-tuple-element.98), channel_id=1, source_target_pairs={{1,0},{2,1},{3,2},{5,4},{6,5},{7,6},{9,8},{10,9},{11,10},{13,12},{... | collective-permute-start | bytes 786440 | tf_op jit(solution)/shard_map/ppermute | solution.py:22
  345.6 8.3 %collective-permute-start.53 = (f32[1,512,128]{2,1,0:T(8,128)S(1)}, f32[1,512,128]{2,1,0:T(8,128)S(1)}, u32[]{:S(2)}, u32[]{:S(2)}) collective-permute-start(f32[1,512,128]{2,1,0:T(8,128)S(1)} %get-tuple-element.97), channel_id=1, source_target_pairs={{0,1},{1,2},{2,3},{4,5},{5,6},{6,7},{8,9},{9,10},{10,11},{12,13},{... | collective-permute-start | bytes 786440 | tf_op jit(solution)/shard_map/ppermute | solution.py:21
  355.1 8.5 %collective-permute-start.54 = (f32[1,512,128]{2,1,0:T(8,128)S(1)}, f32[1,512,128]{2,1,0:T(8,128)S(1)}, u32[]{:S(2)}, u32[]{:S(2)}) collective-permute-start(f32[1,512,128]{2,1,0:T(8,128)S(1)} %get-tuple-element.96), channel_id=1, source_target_pairs={{1,0},{2,1},{3,2},{5,4},{6,5},{7,6},{9,8},{10,9},{11,10},{13,12},{... | collective-permute-start | bytes 786440 | tf_op jit(solution)/shard_map/ppermute | solution.py:22
  356.4 8.3 %collective-permute-start.55 = (f32[1,512,128]{2,1,0:T(8,128)S(1)}, f32[1,512,128]{2,1,0:T(8,128)S(1)}, u32[]{:S(2)}, u32[]{:S(2)}) collective-permute-start(f32[1,512,128]{2,1,0:T(8,128)S(1)} %get-tuple-element.95), channel_id=1, source_target_pairs={{0,1},{1,2},{2,3},{4,5},{5,6},{6,7},{8,9},{9,10},{10,11},{12,13},{... | collective-permute-start | bytes 786440 | tf_op jit(solution)/shard_map/ppermute | solution.py:21
  365.9 8.5 %collective-permute-start.56 = (f32[1,512,128]{2,1,0:T(8,128)S(1)}, f32[1,512,128]{2,1,0:T(8,128)S(1)}, u32[]{:S(2)}, u32[]{:S(2)}) collective-permute-start(f32[1,512,128]{2,1,0:T(8,128)S(1)} %get-tuple-element.94), channel_id=1, source_target_pairs={{1,0},{2,1},{3,2},{5,4},{6,5},{7,6},{9,8},{10,9},{11,10},{13,12},{... | collective-permute-start | bytes 786440 | tf_op jit(solution)/shard_map/ppermute | solution.py:22
  367.2 8.3 %collective-permute-start.57 = (f32[1,512,128]{2,1,0:T(8,128)S(1)}, f32[1,512,128]{2,1,0:T(8,128)S(1)}, u32[]{:S(2)}, u32[]{:S(2)}) collective-permute-start(f32[1,512,128]{2,1,0:T(8,128)S(1)} %get-tuple-element.93), channel_id=1, source_target_pairs={{0,1},{1,2},{2,3},{4,5},{5,6},{6,7},{8,9},{9,10},{10,11},{12,13},{... | collective-permute-start | bytes 786440 | tf_op jit(solution)/shard_map/ppermute | solution.py:21
  376.7 8.7 %collective-permute-start.58 = (f32[1,512,128]{2,1,0:T(8,128)S(1)}, f32[1,512,128]{2,1,0:T(8,128)S(1)}, u32[]{:S(2)}, u32[]{:S(2)}) collective-permute-start(f32[1,512,128]{2,1,0:T(8,128)S(1)} %get-tuple-element.92), channel_id=1, source_target_pairs={{1,0},{2,1},{3,2},{5,4},{6,5},{7,6},{9,8},{10,9},{11,10},{13,12},{... | collective-permute-start | bytes 786440 | tf_op jit(solution)/shard_map/ppermute | solution.py:22
  378.0 8.3 %collective-permute-start.59 = (f32[1,512,128]{2,1,0:T(8,128)S(1)}, f32[1,512,128]{2,1,0:T(8,128)S(1)}, u32[]{:S(2)}, u32[]{:S(2)}) collective-permute-start(f32[1,512,128]{2,1,0:T(8,128)S(1)} %get-tuple-element.91), channel_id=1, source_target_pairs={{0,1},{1,2},{2,3},{4,5},{5,6},{6,7},{8,9},{9,10},{10,11},{12,13},{... | collective-permute-start | bytes 786440 | tf_op jit(solution)/shard_map/ppermute | solution.py:21
  387.8 8.5 %collective-permute-start.60 = (f32[1,512,128]{2,1,0:T(8,128)S(1)}, f32[1,512,128]{2,1,0:T(8,128)S(1)}, u32[]{:S(2)}, u32[]{:S(2)}) collective-permute-start(f32[1,512,128]{2,1,0:T(8,128)S(1)} %get-tuple-element.90), channel_id=1, source_target_pairs={{1,0},{2,1},{3,2},{5,4},{6,5},{7,6},{9,8},{10,9},{11,10},{13,12},{... | collective-permute-start | bytes 786440 | tf_op jit(solution)/shard_map/ppermute | solution.py:22
  398.6 8.5 %collective-permute-start.62 = (f32[1,512,128]{2,1,0:T(8,128)S(1)}, f32[1,512,128]{2,1,0:T(8,128)S(1)}, u32[]{:S(2)}, u32[]{:S(2)}) collective-permute-start(f32[1,512,128]{2,1,0:T(8,128)S(1)} %get-tuple-element.88), channel_id=1, source_target_pairs={{1,0},{2,1},{3,2},{5,4},{6,5},{7,6},{9,8},{10,9},{11,10},{13,12},{... | collective-permute-start | bytes 786440 | tf_op jit(solution)/shard_map/ppermute | solution.py:22
  409.4 8.5 %collective-permute-start.64 = (f32[1,512,128]{2,1,0:T(8,128)S(1)}, f32[1,512,128]{2,1,0:T(8,128)S(1)}, u32[]{:S(2)}, u32[]{:S(2)}) collective-permute-start(f32[1,512,128]{2,1,0:T(8,128)S(1)} %get-tuple-element.86), channel_id=1, source_target_pairs={{1,0},{2,1},{3,2},{5,4},{6,5},{7,6},{9,8},{10,9},{11,10},{13,12},{... | collective-permute-start | bytes 786440 | tf_op jit(solution)/shard_map/ppermute | solution.py:22
  420.2 8.5 %collective-permute-start.66 = (f32[1,512,128]{2,1,0:T(8,128)S(1)}, f32[1,512,128]{2,1,0:T(8,128)S(1)}, u32[]{:S(2)}, u32[]{:S(2)}) collective-permute-start(f32[1,512,128]{2,1,0:T(8,128)S(1)} %get-tuple-element.84), channel_id=1, source_target_pairs={{1,0},{2,1},{3,2},{5,4},{6,5},{7,6},{9,8},{10,9},{11,10},{13,12},{... | collective-permute-start | bytes 786440 | tf_op jit(solution)/shard_map/ppermute | solution.py:22
  431.0 8.5 %collective-permute-start.68 = (f32[1,512,128]{2,1,0:T(8,128)S(1)}, f32[1,512,128]{2,1,0:T(8,128)S(1)}, u32[]{:S(2)}, u32[]{:S(2)}) collective-permute-start(f32[1,512,128]{2,1,0:T(8,128)S(1)} %get-tuple-element.82), channel_id=1, source_target_pairs={{1,0},{2,1},{3,2},{5,4},{6,5},{7,6},{9,8},{10,9},{11,10},{13,12},{... | collective-permute-start | bytes 786440 | tf_op jit(solution)/shard_map/ppermute | solution.py:22
  441.8 8.5 %collective-permute-start.70 = (f32[1,512,128]{2,1,0:T(8,128)S(1)}, f32[1,512,128]{2,1,0:T(8,128)S(1)}, u32[]{:S(2)}, u32[]{:S(2)}) collective-permute-start(f32[1,512,128]{2,1,0:T(8,128)S(1)} %get-tuple-element.80), channel_id=1, source_target_pairs={{1,0},{2,1},{3,2},{5,4},{6,5},{7,6},{9,8},{10,9},{11,10},{13,12},{... | collective-permute-start | bytes 786440 | tf_op jit(solution)/shard_map/ppermute | solution.py:22
  (16 other events, 393.2 us)
Sparse Core Ops, SparseCore 0:
  10.1 51.9 all-gather.1
  455.6 105.8 all-reduce.38
where the time goes:
time: 581 us; the launch traced here: 571 us
  starting transfers between devices  301 us (52%)
  waiting for transfers between devices  199 us (34%)
  other arithmetic  42.4 us (7%)
  between operations  16.9 us (3%)
  local copies, waits for them, and re-layouts  7.08 us (1%)
    ppermute x36, starting transfers between devices, padded_2(): before = lax.ppermute(last, axis, up)  254 us
    unnamed x3, waiting for transfers between devices  105 us
    all_gather x1, waiting for transfers between devices, body(): shard_rows = lax.all_gather(conductivity, 'mesh', axis=1, tiled=True)  54.2 us
    ppermute x36, starting transfers between devices, padded_2(): after = lax.ppermute(leading, axis, down)  46.6 us
    ppermute x36, waiting for transfers between devices, padded_2(): before = lax.ppermute(last, axis, up)  39.1 us
    concatenate x36, other arithmetic, padded_2(): x = jnp.concatenate([before, x, after], axis=dim)  22.2 us
    add x30, other arithmetic, chebyshev(): ratio_next * ratio_now * direct + 2.0 * ratio_next / half_width * remain  15.6 us
  transfers between devices with their start and end apart: 74, of which 38 were waited for; matrix products, arithmetic and copies ran while one was open for 0% of the time, Pallas kernels for 0%

commit v1 on v0

v1 whole, which is shorter than its diff:
```python
import functools

import jax
import jax.numpy as jnp
from jax import lax
from jax.experimental import pallas as pl
from jax.experimental.pallas import tpu as pltpu
from jax.sharding import PartitionSpec as P

STEPS = 3
DEG = 6
LOW = 0.3
HIGH = 15.0
CENTRE = (HIGH + LOW) / 2.0
HALF = (HIGH - LOW) / 2.0
HALO = 40
UNIT = 16
OFF = 56


def weights():
    rho = HALF / CENTRE
    out = []
    for _ in range(DEG):
        new = 1.0 / (2.0 * CENTRE / HALF - rho)
        out.append((new * rho, 2.0 * new / HALF))
        rho = new
    return out


def beside(ref, p, r):
    nx, _, nz = p.shape
    zero = jnp.zeros((1,) + p.shape[1:], p.dtype)
    lane = lax.broadcasted_iota(jnp.int32, p.shape, 2)
    left = jnp.where(lane == 0, 0.0, pltpu.roll(p, 1, 2))
    right = jnp.where(lane == nz - 1, 0.0, pltpu.roll(p, nz - 1, 2))
    total = ref[:, pl.ds(r - 1, UNIT), :] + ref[:, pl.ds(r + 1, UNIT), :]
    total = total + (left + right)
    total = total + jnp.concatenate([zero, p[:-1]], axis=0)
    return total + jnp.concatenate([p[1:], zero], axis=0)


def evolve(rows, sub, n_sub, cond, u0, obs, src, even, odd, us, adj, grad):
    total_apps = 2 * STEPS * DEG
    first = sub == 0
    last = sub == n_sub - 1

    def sweep(app, fn):
        units = -(-(total_apps - app) // UNIT)
        lo = jnp.where(first, 0, -units)
        hi = jnp.where(last, 0, units) + rows // UNIT

        def step(i, carry):
            fn(pl.multiple_of(OFF + i * UNIT, 8))
            return carry

        lax.fori_loop(lo, hi, step, 0)

    def at(ref, r):
        return ref[:, pl.ds(r, UNIT), :]

    def put(ref, r, value):
        ref[:, pl.ds(r, UNIT), :] = value

    def start(r):
        put(src, r, at(cond, r) * at(u0, r))

    sweep(0, start)
    fields = [u0] + list(us)
    w = weights()
    app = 0
    for solve in range(2 * STEPS):
        for k in range(DEG):
            app += 1
            a, b = w[k]

            def one(r, k=k, a=a, b=b, solve=solve):
                c = at(cond, r)
                if k == 0:
                    s = at(src, r)
                    mul = (1.0 + a - 6.0 * b) / CENTRE + b
                    put(even, r, (mul - (b / CENTRE) * c) * s + (b / CENTRE) * beside(src, s, r))
                    return
                here, there = (even, odd) if k % 2 == 1 else (odd, even)
                p = at(here, r)
                s = at(src, r)
                acc = beside(here, p, r) + s + (((1.0 + a) / b - 6.0) - c) * p
                if k == 1:
                    new = b * acc - (a / CENTRE) * s
                else:
                    new = b * acc - a * at(there, r)
                if k < DEG - 1:
                    put(there, r, new)
                    return
                if solve < STEPS:
                    put(fields[solve + 1], r, new)
                    if solve < STEPS - 1:
                        put(src, r, c * new)
                    else:
                        put(src, r, new - obs[STEPS - 1, :, pl.ds(r, UNIT), :])
                    return
                n = 2 * STEPS - solve
                older = at(fields[n - 1], r)
                add = new * (older - at(fields[n], r))
                if n == STEPS:
                    put(grad, r, add)
                else:
                    put(grad, r, at(grad, r) + add)
                if n > 1:
                    put(src, r, older - obs[n - 2, :, pl.ds(r, UNIT), :] + c * new)

            sweep(app, one)


def choose(x, ids):
    rows = [lax.dynamic_index_in_dim(x, ids[i], 0, keepdims=True) for i in range(ids.shape[0])]
    return jnp.concatenate(rows, axis=0)


def local_kernel(n_sub, rows, c_ref, u_ref, o_ref, last_ref, g_ref, cond, u0, obs, src, even, odd, u1, u2, u3, grad):
    sub = lax.axis_index("sub")
    wide = rows + 2 * HALO
    for ref in (src, even, odd):
        ref[...] = jnp.zeros_like(ref)
    window = pl.ds(OFF - HALO, wide)
    cond[:, window, :] = c_ref[...]
    u0[:, window, :] = u_ref[...]
    obs[:, :, window, :] = o_ref[...]
    evolve(rows, sub, n_sub, cond, u0, obs, src, even, odd, (u1, u2, u3), None, grad)
    last_ref[...] = u3[:, pl.ds(OFF, rows), :]
    g_ref[...] = grad[:, pl.ds(OFF, rows), :]


def body(conductivity, footprint, initial, observed):
    n_mesh = lax.axis_size("mesh")
    n_sub = lax.axis_size("sub")
    me = lax.axis_index("mesh")
    _, per_owner, depth, block_y, nz = conductivity.shape
    tiles = footprint.shape[1]
    ny = tiles * block_y
    rows = ny // n_sub
    nx = depth * n_sub

    owners = footprint // per_owner
    local = footprint % per_owner
    mine = owners == me
    wanted = jnp.sum(jnp.where(mine, local, 0), axis=1)
    has = jnp.any(mine, axis=1)
    send = choose(conductivity[0], wanted)
    got = lax.all_to_all(send, "mesh", 0, 0, tiled=True)
    my_owners = lax.dynamic_index_in_dim(owners, me, 0, keepdims=False)
    picked = choose(got, my_owners)
    cond = jnp.transpose(picked, (1, 0, 2, 3)).reshape(depth, ny, nz)

    def spread(x):
        pads = [(0, 0)] * (x.ndim - 2) + [(HALO, HALO), (0, 0)]
        x = jnp.pad(x, pads)
        parts = [lax.slice_in_dim(x, s * rows, (s + 1) * rows + 2 * HALO, axis=x.ndim - 2) for s in range(n_sub)]
        y = lax.all_to_all(jnp.stack(parts), "sub", 0, 0, tiled=True)
        y = jnp.moveaxis(y, 0, -4)
        return y.reshape(y.shape[:-4] + (nx,) + y.shape[-2:])

    o = spread(observed[0])
    cu = spread(jnp.stack([cond, initial[0]]))

    full = pltpu.VMEM((nx, rows + 2 * OFF, nz), jnp.float32)
    vm = pl.BlockSpec(memory_space=pltpu.VMEM)
    out = jax.ShapeDtypeStruct((nx, rows, nz), jnp.float32)
    final, grad = pl.pallas_call(
        functools.partial(local_kernel, n_sub, rows),
        out_shape=(out, out),
        in_specs=[vm] * 3,
        out_specs=(vm, vm),
        scratch_shapes=[full, full, pltpu.VMEM((STEPS, nx, rows + 2 * OFF, nz), jnp.float32)] + [full] * 7,
        compiler_params=pltpu.CompilerParams(vmem_limit_bytes=48 * 1024 * 1024),
    )(cu[0], cu[1], o)

    def collect(x):
        y = lax.all_to_all(x, "sub", 0, 0, tiled=True)
        y = y.reshape(n_sub, depth, rows, nz)
        return jnp.transpose(y, (1, 0, 2, 3)).reshape(depth, ny, nz)

    g = collect(grad)
    final_field = collect(final)
    g_tiles = jnp.transpose(g.reshape(depth, tiles, block_y, nz), (1, 0, 2, 3))
    hit = my_owners[None, :] == jnp.arange(n_mesh, dtype=jnp.int32)[:, None]
    which = jnp.sum(jnp.where(hit, jnp.arange(tiles, dtype=jnp.int32)[None, :], 0), axis=1)
    back = lax.all_to_all(choose(g_tiles, which), "mesh", 0, 0, tiled=True)
    keep = (wanted[None, :] == jnp.arange(per_owner, dtype=jnp.int32)[:, None]) & has[None, :]
    gradient = jnp.sum(jnp.where(keep[:, :, None, None, None], back[None], 0.0), axis=1)
    return gradient[None], final_field[None]


def solution(mesh):
    return jax.shard_map(
        body,
        mesh=mesh,
        in_specs=(
            P("sub", "mesh", None, None, None),
            P(),
            P("mesh", "sub", None, None),
            P("mesh", None, "sub", None, None),
        ),
        out_specs=(P("sub", "mesh", None, None, None), P("mesh", "sub", None, None)),
        check_vma=False,
    )
```

time: 581 us -> 209 us (0.36); the launches traced: 571 us -> 208 us
  starting transfers between devices: 301 us -> 30.4 us
  waiting for transfers between devices: 199 us -> 61.7 us
  Pallas kernels: 0 us -> 39.8 us
  other arithmetic: 42.4 us -> 6.91 us
  between operations: 16.9 us -> 45.4 us
  local copies, waits for them, and re-layouts: 7.08 us -> 23.6 us
    ppermute x72 -> x0, starting transfers between devices: 301 us -> none  [the longest x36 254 us: padded_2(): before = lax.ppermute(last, axis, up)]
    unnamed x3 -> x0, waiting for transfers between devices: 105 us -> none
    all_to_all x0 -> x6, waiting for transfers between devices: none -> 61.7 us  [the longest x2 32 us: spread(): y = lax.all_to_all(jnp.stack(parts), 'sub', 0, 0, tiled=True)]
    all_gather x1 -> x0, waiting for transfers between devices: 54.2 us -> none  [body(): shard_rows = lax.all_gather(conductivity, 'mesh', axis=1, tiled=True)]
    pallas_call x0 -> x1, Pallas kernels: none -> 39.8 us  [body(): pl.pallas_call(functools.partial(local_kernel, n_sub, rows), out_shape=(o...]
    ppermute x72 -> x0, waiting for transfers between devices: 39.2 us -> none  [the longest x36 39.1 us: padded_2(): before = lax.ppermute(last, axis, up)]
    all_to_all x0 -> x6, starting transfers between devices: none -> 30.4 us  [the longest x2 11.5 us: collect(): y = lax.all_to_all(x, 'sub', 0, 0, tiled=True)]
    concatenate x36 -> x0, other arithmetic: 22.2 us -> none  [padded_2(): x = jnp.concatenate([before, x, after], axis=dim)]
  transfers between devices with their start and end apart: 74 -> 6, of which waited for: 38 -> 5; matrix products, arithmetic and copies ran while one was open for 0% -> 7% of each run, Pallas kernels for 0% -> 0%
where the time goes in v1:
time: 209 us; the launch traced here: 208 us
  waiting for transfers between devices  61.7 us (30%)
  between operations  45.4 us (22%)
  Pallas kernels  39.8 us (19%)
  starting transfers between devices  30.4 us (15%)
  local copies, waits for them, and re-layouts  23.6 us (11%)
  other arithmetic  6.91 us (3%)
    pallas_call x1, Pallas kernels, body(): pl.pallas_call(functools.partial(local_kernel, n_sub, rows), out_shape=(o...  39.8 us
    all_to_all x2, waiting for transfers between devices, spread(): y = lax.all_to_all(jnp.stack(parts), 'sub', 0, 0, tiled=True)  32 us
    unnamed x27, local copies, waits for them, and re-layouts  14.9 us
    all_to_all x1, waiting for transfers between devices, body(): back = lax.all_to_all(choose(g_tiles, which), 'mesh', 0, 0, tiled=True)  13.4 us
    all_to_all x1, waiting for transfers between devices, body(): got = lax.all_to_all(send, 'mesh', 0, 0, tiled=True)  12.5 us
    all_to_all x2, starting transfers between devices, collect(): y = lax.all_to_all(x, 'sub', 0, 0, tiled=True)  11.5 us
    all_to_all x2, starting transfers between devices, spread(): y = lax.all_to_all(jnp.stack(parts), 'sub', 0, 0, tiled=True)  8.02 us
    all_to_all x1, starting transfers between devices, body(): got = lax.all_to_all(send, 'mesh', 0, 0, tiled=True)  7.25 us
  transfers between devices with their start and end apart: 6, of which 5 were waited for; matrix products, arithmetic and copies ran while one was open for 7% of the time, Pallas kernels for 0%

profile of v1, /device:TPU:0, one launch (start us, length us, event | category | flops | bytes accessed | tf_op | source)
XLA Modules:
  0.0 207.8 jit_solution(13440976432011595336)
XLA Ops:
  0.6 0.0 copy-start.1
  0.6 0.9 fusion.13
  1.6 0.8 fusion.9
  2.4 0.7 fusion.17
  13.7 1.5 bitcast_dynamic-update-slice_fusion.23
  15.9 1.5 bitcast_dynamic-update-slice_fusion.22
  17.9 1.5 bitcast_dynamic-update-slice_fusion.21
  20.0 1.5 bitcast_dynamic-update-slice_fusion.20
  22.1 1.5 bitcast_dynamic-update-slice_fusion.19
  24.3 1.5 bitcast_dynamic-update-slice_fusion.18
  26.3 1.5 bitcast_dynamic-update-slice_fusion.17
  28.4 1.5 bitcast_dynamic-update-slice_fusion.16
  29.9 7.3 %all-to-all-start = ((f32[8,2,64,128]{3,2,1,0:T(8,128)}), f32[8,2,64,128]{3,2,1,0:T(8,128)S(1)}, u32[]{:S(2)}, u32[]{:S(2)}) async-start(f32[8,2,64,128]{3,2,1,0:T(8,128)} %bitcast_dynamic-update-slice_fusion.16), calls=%async_computation | async-start | bytes 1048576 | tf_op jit(solution)/shard_map/all_to_all | solution.py:150
  37.2 0.0 copy-done.1
  37.2 0.2 fusion
  37.4 1.7 pad_maximum_fusion
  39.1 12.5 %all-to-all-done = f32[8,2,64,128]{3,2,1,0:T(8,128)S(1)} async-done(((f32[8,2,64,128]{3,2,1,0:T(8,128)}), f32[8,2,64,128]{3,2,1,0:T(8,128)S(1)}, u32[]{:S(2)}, u32[]{:S(2)}) %all-to-all-start) | async-done | bytes 524320 | tf_op jit(solution)/shard_map/all_to_all | solution.py:150
  51.7 3.6 %all-to-all-start.2 = ((f32[4,3,2,208,128]{4,3,2,1,0:T(8,128)}), f32[4,3,2,208,128]{4,3,2,1,0:T(8,128)S(1)}, u32[]{:S(2)}, u32[]{:S(2)}) async-start(f32[4,3,2,208,128]{4,3,2,1,0:T(8,128)} %pad_maximum_fusion), calls=%async_computation.2 | async-start | bytes 5111808 | tf_op jit(solution)/shard_map/all_to_all | solution.py:159
  55.3 0.7 fusion.16
  70.8 0.0 copy-start.2
  71.0 1.1 fusion.5
  72.1 0.0 copy-done.2
  72.1 0.1 pad_maximum_fusion.2
  72.1 0.1 fusion.2
  72.2 1.3 pad_maximum_fusion.1
  73.5 12.4 %all-to-all-done.2 = f32[4,3,2,208,128]{4,3,2,1,0:T(8,128)S(1)} async-done(((f32[4,3,2,208,128]{4,3,2,1,0:T(8,128)}), f32[4,3,2,208,128]{4,3,2,1,0:T(8,128)S(1)}, u32[]{:S(2)}, u32[]{:S(2)}) %all-to-all-start.2) | async-done | bytes 2555936 | tf_op jit(solution)/shard_map/all_to_all | solution.py:159
  85.9 0.0 copy-start
  85.9 4.4 %all-to-all-start.1 = ((f32[4,2,2,208,128]{4,3,2,1,0:T(8,128)}), f32[4,2,2,208,128]{4,3,2,1,0:T(8,128)}, u32[]{:S(2)}, u32[]{:S(2)}) async-start(f32[4,2,2,208,128]{4,3,2,1,0:T(8,128)} %pad_maximum_fusion.1), calls=%async_computation.1 | async-start | bytes 3407872 | tf_op jit(solution)/shard_map/all_to_all | solution.py:159
  90.3 0.0 copy-done
  90.3 1.9 copy.33
  92.2 19.6 %all-to-all-done.1 = f32[4,2,2,208,128]{4,3,2,1,0:T(8,128)} async-done(((f32[4,2,2,208,128]{4,3,2,1,0:T(8,128)}), f32[4,2,2,208,128]{4,3,2,1,0:T(8,128)}, u32[]{:S(2)}, u32[]{:S(2)}) %all-to-all-start.1) | async-done | bytes 1703968 | tf_op jit(solution)/shard_map/all_to_all | solution.py:159
  111.8 1.5 fusion.14
  113.4 39.8 %shard_map.59 = (f32[8,128,128]{2,1,0:T(8,128)}, f32[8,128,128]{2,1,0:T(8,128)}) custom-call(f32[8,208,128]{2,1,0:T(8,128)S(1)} %bitcast.110, f32[8,208,128]{2,1,0:T(8,128)S(1)} %bitcast.109, f32[3,8,208,128]{3,2,1,0:T(8,128)S(1)} %bitcast.108), custom_call_target="tpu_custom_call" | custom-call | tf_op jit(solution)/shard_map/pallas_call | solution.py:169
  153.2 8.0 %all-to-all-start.3 = ((f32[8,128,128]{2,1,0:T(8,128)}), f32[8,128,128]{2,1,0:T(8,128)S(1)}, u32[]{:S(2)}, u32[]{:S(2)}) async-start(f32[8,128,128]{2,1,0:T(8,128)} %get-tuple-element.4), calls=%async_computation.3 | async-start | bytes 1048576 | tf_op jit(solution)/shard_map/all_to_all | solution.py:179
  161.2 0.7 fusion.15
  176.7 0.0 all-to-all-done.3
  176.7 3.5 %all-to-all-start.5 = ((f32[8,128,128]{2,1,0:T(8,128)}), f32[8,128,128]{2,1,0:T(8,128)S(1)}, u32[]{:S(2)}, u32[]{:S(2)}) async-start(f32[8,128,128]{2,1,0:T(8,128)} %get-tuple-element.5), calls=%async_computation.5 | async-start | bytes 1048576 | tf_op jit(solution)/shard_map/all_to_all | solution.py:179
  180.2 0.6 bitcast_dynamic-update-slice_fusion.15
  180.9 0.6 bitcast_dynamic-update-slice_fusion.14
  181.5 0.6 bitcast_dynamic-update-slice_fusion.13
  182.1 0.6 bitcast_dynamic-update-slice_fusion.12
  182.8 0.6 bitcast_dynamic-update-slice_fusion.11
  183.4 0.6 bitcast_dynamic-update-slice_fusion.10
  184.0 0.6 bitcast_dynamic-update-slice_fusion.9
  184.6 0.6 bitcast_dynamic-update-slice_fusion.8
  185.2 3.8 %all-to-all-done.5 = f32[8,128,128]{2,1,0:T(8,128)S(1)} async-done(((f32[8,128,128]{2,1,0:T(8,128)}), f32[8,128,128]{2,1,0:T(8,128)S(1)}, u32[]{:S(2)}, u32[]{:S(2)}) %all-to-all-start.5) | async-done | bytes 524320 | tf_op jit(solution)/shard_map/all_to_all | solution.py:179
  189.0 3.6 %all-to-all-start.4 = ((f32[8,2,64,128]{3,2,1,0:T(8,128)}), f32[8,2,64,128]{3,2,1,0:T(8,128)S(1)}, u32[]{:S(2)}, u32[]{:S(2)}) async-start(f32[8,2,64,128]{3,2,1,0:T(8,128)} %bitcast_dynamic-update-slice_fusion.8), calls=%async_computation.4 | async-start | bytes 1048576 | tf_op jit(solution)/shard_map/all_to_all | solution.py:188
  192.7 0.8 copy.35
  193.5 13.4 %all-to-all-done.4 = f32[8,2,64,128]{3,2,1,0:T(8,128)S(1)} async-done(((f32[8,2,64,128]{3,2,1,0:T(8,128)}), f32[8,2,64,128]{3,2,1,0:T(8,128)S(1)}, u32[]{:S(2)}, u32[]{:S(2)}) %all-to-all-start.4) | async-done | bytes 524320 | tf_op jit(solution)/shard_map/all_to_all | solution.py:188
  206.9 0.9 select_reduce_fusion
  (12 shorter events, 0.2 us)
Async XLA Ops:
  0.6 36.5 %copy-start.1 = (f32[1,3,2,512,128]{4,3,2,1,0:T(8,128)S(1)}, f32[1,3,2,512,128]{4,3,2,1,0:T(8,128)}, u32[]{:S(2)}) copy-start(f32[1,3,2,512,128]{4,3,2,1,0:T(8,128)} %param.7) | copy-start | bytes 4718596
  29.9 21.7 %all-to-all-start = ((f32[8,2,64,128]{3,2,1,0:T(8,128)}), f32[8,2,64,128]{3,2,1,0:T(8,128)S(1)}, u32[]{:S(2)}, u32[]{:S(2)}) async-start(f32[8,2,64,128]{3,2,1,0:T(8,128)} %bitcast_dynamic-update-slice_fusion.16), calls=%async_computation | async-start | bytes 1048576 | tf_op jit(solution)/shard_map/all_to_all | solution.py:150
  51.7 34.2 %all-to-all-start.2 = ((f32[4,3,2,208,128]{4,3,2,1,0:T(8,128)}), f32[4,3,2,208,128]{4,3,2,1,0:T(8,128)S(1)}, u32[]{:S(2)}, u32[]{:S(2)}) async-start(f32[4,3,2,208,128]{4,3,2,1,0:T(8,128)} %pad_maximum_fusion), calls=%async_computation.2 | async-start | bytes 5111808 | tf_op jit(solution)/shard_map/all_to_all | solution.py:159
  70.8 1.3 copy-start.2
  85.9 4.4 %copy-start = (f32[4,3,2,208,128]{4,3,2,1,0:T(8,128)}, f32[4,3,2,208,128]{4,3,2,1,0:T(8,128)S(1)}, u32[]{:S(2)}) copy-start(f32[4,3,2,208,128]{4,3,2,1,0:T(8,128)S(1)} %all-to-all-done.2) | copy-start | bytes 7667716
  85.9 25.9 %all-to-all-start.1 = ((f32[4,2,2,208,128]{4,3,2,1,0:T(8,128)}), f32[4,2,2,208,128]{4,3,2,1,0:T(8,128)}, u32[]{:S(2)}, u32[]{:S(2)}) async-start(f32[4,2,2,208,128]{4,3,2,1,0:T(8,128)} %pad_maximum_fusion.1), calls=%async_computation.1 | async-start | bytes 3407872 | tf_op jit(solution)/shard_map/all_to_all | solution.py:159
  153.2 23.5 %all-to-all-start.3 = ((f32[8,128,128]{2,1,0:T(8,128)}), f32[8,128,128]{2,1,0:T(8,128)S(1)}, u32[]{:S(2)}, u32[]{:S(2)}) async-start(f32[8,128,128]{2,1,0:T(8,128)} %get-tuple-element.4), calls=%async_computation.3 | async-start | bytes 1048576 | tf_op jit(solution)/shard_map/all_to_all | solution.py:179
  176.7 12.3 %all-to-all-start.5 = ((f32[8,128,128]{2,1,0:T(8,128)}), f32[8,128,128]{2,1,0:T(8,128)S(1)}, u32[]{:S(2)}, u32[]{:S(2)}) async-start(f32[8,128,128]{2,1,0:T(8,128)} %get-tuple-element.5), calls=%async_computation.5 | async-start | bytes 1048576 | tf_op jit(solution)/shard_map/all_to_all | solution.py:179
  189.0 17.8 %all-to-all-start.4 = ((f32[8,2,64,128]{3,2,1,0:T(8,128)}), f32[8,2,64,128]{3,2,1,0:T(8,128)S(1)}, u32[]{:S(2)}, u32[]{:S(2)}) async-start(f32[8,2,64,128]{3,2,1,0:T(8,128)} %bitcast_dynamic-update-slice_fusion.8), calls=%async_computation.4 | async-start | bytes 1048576 | tf_op jit(solution)/shard_map/all_to_all | solution.py:188

commit v2 on v1

v2 whole, which is shorter than its diff:
```python
import functools

import jax
import jax.numpy as jnp
from jax import lax
from jax.experimental import pallas as pl
from jax.experimental.pallas import tpu as pltpu
from jax.sharding import PartitionSpec as P

STEPS = 3
DEG = 6
LOW = 0.3
HIGH = 15.0
CENTRE = (HIGH + LOW) / 2.0
HALF = (HIGH - LOW) / 2.0
HALO = 40
UNIT = 16
MESH = pl.DeviceIdType.MESH
OFF = 88


def weights():
    rho = HALF / CENTRE
    out = []
    for _ in range(DEG):
        new = 1.0 / (2.0 * CENTRE / HALF - rho)
        out.append((new * rho, 2.0 * new / HALF))
        rho = new
    return out


def beside(ref, p, r):
    nx, _, nz = p.shape
    zero = jnp.zeros((1,) + p.shape[1:], p.dtype)
    lane = lax.broadcasted_iota(jnp.int32, p.shape, 2)
    left = jnp.where(lane == 0, 0.0, pltpu.roll(p, 1, 2))
    right = jnp.where(lane == nz - 1, 0.0, pltpu.roll(p, nz - 1, 2))
    total = ref[:, pl.ds(r - 1, UNIT), :] + ref[:, pl.ds(r + 1, UNIT), :]
    total = total + (left + right)
    total = total + jnp.concatenate([zero, p[:-1]], axis=0)
    return total + jnp.concatenate([p[1:], zero], axis=0)


def evolve(rows, sub, n_sub, cond, u0, obs, src, even, odd, us, grad, need_obs, forward_done):
    total_apps = 2 * STEPS * DEG
    first = sub == 0
    last = sub == n_sub - 1

    def sweep(app, fn):
        units = -(-(total_apps - app) // UNIT)
        lo = jnp.where(first, 0, -units)
        hi = jnp.where(last, 0, units) + rows // UNIT

        def step(i, carry):
            fn(pl.multiple_of(OFF + i * UNIT, 8))
            return carry

        lax.fori_loop(lo, hi, step, 0)

    def at(ref, r):
        return ref[:, pl.ds(r, UNIT), :]

    def put(ref, r, value):
        ref[:, pl.ds(r, UNIT), :] = value

    def start(r):
        put(src, r, at(cond, r) * at(u0, r))

    sweep(0, start)
    fields = [u0] + list(us)
    w = weights()
    app = 0
    for solve in range(2 * STEPS):
        for k in range(DEG):
            app += 1
            a, b = w[k]

            def one(r, k=k, a=a, b=b, solve=solve):
                c = at(cond, r)
                if k == 0:
                    s = at(src, r)
                    mul = (1.0 + a - 6.0 * b) / CENTRE + b
                    put(even, r, (mul - (b / CENTRE) * c) * s + (b / CENTRE) * beside(src, s, r))
                    return
                here, there = (even, odd) if k % 2 == 1 else (odd, even)
                p = at(here, r)
                s = at(src, r)
                acc = beside(here, p, r) + s + (((1.0 + a) / b - 6.0) - c) * p
                if k == 1:
                    new = b * acc - (a / CENTRE) * s
                else:
                    new = b * acc - a * at(there, r)
                if k < DEG - 1:
                    put(there, r, new)
                    return
                if solve < STEPS:
                    put(fields[solve + 1], r, new)
                    if solve < STEPS - 1:
                        put(src, r, c * new)
                    else:
                        put(src, r, new - obs[STEPS - 1, :, pl.ds(r, UNIT), :])
                    return
                n = 2 * STEPS - solve
                older = at(fields[n - 1], r)
                add = new * (older - at(fields[n], r))
                if n == STEPS:
                    put(grad, r, add)
                else:
                    put(grad, r, at(grad, r) + add)
                if n > 1:
                    put(src, r, older - obs[n - 2, :, pl.ds(r, UNIT), :] + c * new)

            if k == DEG - 1 and STEPS - 1 <= solve < 2 * STEPS - 1:
                need_obs(2 * STEPS - 2 - solve)
            sweep(app, one)
        if solve == STEPS - 1:
            forward_done()


def whole_kernel(n_mesh, n_sub, rows, foot, c_ref, u_ref, o_ref, grad_ref, last_ref, send_c, got_c, layer, cond, u0, obs,
                 src, even, odd, u1, u2, u3, grad, tiles_g, send_g, got_g,
                 mesh_send, mesh_recv, back_send, back_recv, sub_send, sub_recv, near):
    sub = lax.axis_index("sub")
    me = lax.axis_index("mesh")
    per_owner, depth, block_y, nz = c_ref.shape[1:]
    tiles = foot.shape[1]
    ny = tiles * block_y
    per_dev = tiles // n_sub
    f_u, f_c, f_last, f_g = STEPS, STEPS + 1, STEPS + 2, STEPS + 3

    barrier = pltpu.get_barrier_semaphore()
    for d in range(1, n_sub):
        pl.semaphore_signal(barrier, inc=1, device_id={"sub": lax.rem(sub + d, n_sub)}, device_id_type=MESH)
    for d in range(1, n_mesh):
        pl.semaphore_signal(barrier, inc=1, device_id={"mesh": lax.rem(me + d, n_mesh)}, device_id_type=MESH)

    base = me * per_owner
    slot, known, tile_of = [], [], []
    for d in range(n_mesh):
        m = lax.rem(me + d, n_mesh)
        pick = jnp.int32(0)
        has = jnp.int32(0)
        for t in range(tiles):
            rel = foot[m, t] - base
            inside = (rel >= 0) & (rel < per_owner)
            pick = jnp.where(inside, rel, pick)
            has = jnp.where(inside, 1, has)
        slot.append(pick)
        known.append(has)
        mine = jnp.int32(0)
        for t in range(tiles):
            rel = foot[me, t] - m * per_owner
            mine = jnp.where((rel >= 0) & (rel < per_owner), t, mine)
        tile_of.append(mine)

    pl.semaphore_wait(barrier, n_sub + n_mesh - 2)

    def mesh_copy(d, send, got, ss, rs):
        return pltpu.make_async_remote_copy(
            src_ref=send.at[d], dst_ref=got.at[me], send_sem=ss.at[d], recv_sem=rs.at[d],
            device_id={"mesh": lax.rem(me + d, n_mesh)}, device_id_type=MESH)

    out_c = []
    for d in range(1, n_mesh):
        send_c[d] = c_ref[0, slot[d]]
        out_c.append(mesh_copy(d, send_c, got_c, mesh_send, mesh_recv))
        out_c[-1].start()
    got_c[me] = c_ref[0, slot[0]]

    def spread(f, source, target, halo):
        wide = rows + 2 * halo
        copies = []
        for d in [1, 2, 3, 0] if n_sub == 4 else list(range(n_sub)):
            to = lax.rem(sub + d, n_sub)
            begin = jnp.clip(to * rows - halo, 0, ny - wide)
            begin = pl.multiple_of(begin, 8)
            land = pl.multiple_of(OFF + begin - to * rows, 8)
            from_ref = source.at[:, pl.ds(begin, wide), :]
            to_ref = target.at[pl.ds(depth * sub, depth), pl.ds(land, wide), :]
            if d == 0:
                copy = pltpu.make_async_copy(from_ref, to_ref, near.at[f])
            else:
                copy = pltpu.make_async_remote_copy(
                    src_ref=from_ref, dst_ref=to_ref, send_sem=sub_send.at[f, d], recv_sem=sub_recv.at[f, d],
                    device_id={"sub": to}, device_id_type=MESH)
            copy.start()
            copies.append((d, copy))
        return copies

    def arrive(copies):
        for d, copy in copies:
            if d == 0:
                copy.wait()
            else:
                copy.wait_recv()

    halos = [-(-(DEG * n) // 8) * 8 for n in range(1, STEPS + 1)]
    ready = {}
    ready["u"] = spread(f_u, u_ref.at[0], u0, HALO)
    ready[STEPS - 1] = spread(STEPS - 1, o_ref.at[0, STEPS - 1], obs.at[STEPS - 1], halos[STEPS - 1])

    for ref in (src, even, odd):
        ref[...] = jnp.zeros_like(ref)

    for copy in out_c:
        copy.wait_recv()
    for t in range(tiles):
        owner = lax.div(foot[me, t], jnp.int32(per_owner))
        layer[:, t * block_y:(t + 1) * block_y, :] = got_c[owner]
    ready["c"] = spread(f_c, layer, cond, HALO)
    for n in range(STEPS - 2, -1, -1):
        ready[n] = spread(n, o_ref.at[0, n], obs.at[n], halos[n])
    arrive(ready["u"])
    arrive(ready["c"])

    def forward_done():
        copies = []
        for d in range(n_sub):
            to = lax.rem(sub + d, n_sub)
            from_ref = u3.at[pl.ds(depth * to, depth), pl.ds(OFF, rows), :]
            to_ref = last_ref.at[0, :, pl.ds(sub * rows, rows), :]
            if d == 0:
                copy = pltpu.make_async_copy(from_ref, to_ref, near.at[f_last])
            else:
                copy = pltpu.make_async_remote_copy(
                    src_ref=from_ref, dst_ref=to_ref, send_sem=sub_send.at[f_last, d],
                    recv_sem=sub_recv.at[f_last, d], device_id={"sub": to}, device_id_type=MESH)
            copy.start()
            copies.append((d, copy))
        ready["last"] = copies

    evolve(rows, sub, n_sub, cond, u0, obs, src, even, odd, (u1, u2, u3), grad,
           lambda n: arrive(ready[n]), forward_done)

    copies = []
    for d in list(range(1, n_sub)) + [0]:
        to = lax.rem(sub + d, n_sub)
        for j in range(per_dev):
            from_ref = grad.at[pl.ds(depth * to, depth), pl.ds(OFF + j * block_y, block_y), :]
            to_ref = tiles_g.at[sub * per_dev + j]
            f = f_g + j
            if d == 0:
                copy = pltpu.make_async_copy(from_ref, to_ref, near.at[f])
            else:
                copy = pltpu.make_async_remote_copy(
                    src_ref=from_ref, dst_ref=to_ref, send_sem=sub_send.at[f, d], recv_sem=sub_recv.at[f, d],
                    device_id={"sub": to}, device_id_type=MESH)
            copy.start()
            copies.append((d, copy))
    ready["g"] = copies
    arrive(copies)

    out_g = []
    for d in range(1, n_mesh):
        send_g[d] = tiles_g[tile_of[d]]
        out_g.append(mesh_copy(d, send_g, got_g, back_send, back_recv))
        out_g[-1].start()
    got_g[me] = tiles_g[tile_of[0]]
    for copy in out_g:
        copy.wait_recv()
    for b in range(per_owner):
        total = jnp.zeros((depth, block_y, nz), jnp.float32)
        for d in range(n_mesh):
            use = (slot[d] == b) & (known[d] == 1)
            total = total + jnp.where(use, got_g[lax.rem(me + d, n_mesh)], 0.0)
        grad_ref[0, b] = total

    arrive(ready["last"])
    for copies in ready.values():
        for d, copy in copies:
            if d:
                copy.wait_send()
    for copy in out_c + out_g:
        copy.wait_send()


def body(conductivity, footprint, initial, observed):
    n_mesh = lax.axis_size("mesh")
    n_sub = lax.axis_size("sub")
    _, per_owner, depth, block_y, nz = conductivity.shape
    tiles = footprint.shape[1]
    ny = tiles * block_y
    rows = ny // n_sub
    nx = depth * n_sub
    per_dev = tiles // n_sub

    def vmem(*shape):
        return pltpu.VMEM(shape, jnp.float32)

    full = vmem(nx, rows + 2 * OFF, nz)
    blocks = vmem(n_mesh, depth, block_y, nz)
    dma = pltpu.SemaphoreType.DMA
    fields = STEPS + 3 + per_dev
    vm = pl.BlockSpec(memory_space=pltpu.VMEM)
    hbm = pl.BlockSpec(memory_space=pl.ANY)
    return pl.pallas_call(
        functools.partial(whole_kernel, n_mesh, n_sub, rows),
        out_shape=(
            jax.ShapeDtypeStruct(conductivity.shape, jnp.float32),
            jax.ShapeDtypeStruct(initial.shape, jnp.float32),
        ),
        in_specs=[pl.BlockSpec(memory_space=pltpu.SMEM), vm, hbm, hbm],
        out_specs=(vm, hbm),
        scratch_shapes=[blocks, blocks, vmem(depth, ny, nz), full, full, vmem(STEPS, nx, rows + 2 * OFF, nz)]
        + [full] * 7
        + [vmem(tiles, depth, block_y, nz), blocks, blocks]
        + [dma((n_mesh,))] * 4
        + [dma((fields, n_sub))] * 2
        + [dma((fields,))],
        compiler_params=pltpu.CompilerParams(
            collective_id=0, has_side_effects=True, vmem_limit_bytes=48 * 1024 * 1024
        ),
    )(footprint, conductivity, initial, observed)


def solution(mesh):
    return jax.shard_map(
        body,
        mesh=mesh,
        in_specs=(
            P("sub", "mesh", None, None, None),
            P(),
            P("mesh", "sub", None, None),
            P("mesh", None, "sub", None, None),
        ),
        out_specs=(P("sub", "mesh", None, None, None), P("mesh", "sub", None, None)),
        check_vma=False,
    )
```

time: 209 us -> 102 us (0.49)
  the two profiles are of different devices: /device:TPU:0 before, /device:TPU:15 now
where the time goes in v2:
time: 102 us
  Pallas kernels  95.7 us (94%)
  local copies, waits for them, and re-layouts  5.58 us (5%)
    pallas_call x1, Pallas kernels, body(): pl.pallas_call(functools.partial(whole_kernel, n_mesh, n_sub, rows), out_...  95.7 us
    unnamed x10, local copies, waits for them, and re-layouts  5.58 us

profile of v2, /device:TPU:15, one launch (start us, length us, event | category | flops | bytes accessed | tf_op | source)
XLA Modules:
  0.0 101.9 jit_solution(2295974436438388437)
XLA Ops:
  0.6 0.0 copy-start
  0.6 1.4 %copy-done = f32[1,3,2,512,128]{4,3,2,1,0:T(8,128)S(1)} copy-done((f32[1,3,2,512,128]{4,3,2,1,0:T(8,128)S(1)}, f32[1,3,2,512,128]{4,3,2,1,0:T(8,128)}, u32[]{:S(2)}) %copy-start) | copy-done | bytes 1572888
  2.0 0.0 copy-start.1
  2.0 1.0 %copy-done.1 = f32[1,2,512,128]{3,2,1,0:T(8,128)S(1)} copy-done((f32[1,2,512,128]{3,2,1,0:T(8,128)S(1)}, f32[1,2,512,128]{3,2,1,0:T(8,128)}, u32[]{:S(2)}) %copy-start.1) | copy-done | bytes 524312
  3.1 0.0 copy-start.2
  3.1 0.9 copy-done.2
  4.0 0.0 copy-start.3
  4.0 0.7 copy-done.3
  4.7 95.7 %shard_map.59 = (f32[1,4,2,64,128]{4,3,2,1,0:T(8,128)S(1)}, f32[1,2,512,128]{3,2,1,0:T(8,128)S(1)}) custom-call(s32[8,8]{1,0:T(8,128)S(1)} %copy-done.3, f32[1,4,2,64,128]{4,3,2,1,0:T(8,128)S(1)} %copy-done.2, f32[1,2,512,128]{3,2,1,0:T(8,128)S(1)} %copy-done.1, f32[1,3,2,512,128]{4,3,2,1,0:T(8,128)S(1)} %copy-done), custom_call_target="tpu_custom_call" | custom-call | tf_op jit(solution)/shard_map/pallas_call | solution.py:296
  100.4 0.7 copy.8
  101.1 0.8 copy.9
Async XLA Ops:
  0.6 1.4 %copy-start = (f32[1,3,2,512,128]{4,3,2,1,0:T(8,128)S(1)}, f32[1,3,2,512,128]{4,3,2,1,0:T(8,128)}, u32[]{:S(2)}) copy-start(f32[1,3,2,512,128]{4,3,2,1,0:T(8,128)} %o_ref.1) | copy-start | bytes 4718596
  2.0 1.0 %copy-start.1 = (f32[1,2,512,128]{3,2,1,0:T(8,128)S(1)}, f32[1,2,512,128]{3,2,1,0:T(8,128)}, u32[]{:S(2)}) copy-start(f32[1,2,512,128]{3,2,1,0:T(8,128)} %u_ref.1) | copy-start | bytes 1572868
  3.1 0.9 copy-start.2
  4.0 0.7 copy-start.3

commit v3 on v2

--- a/solution.py
+++ b/solution.py
@@ -14,7 +14,7 @@
 CENTRE = (HIGH + LOW) / 2.0
 HALF = (HIGH - LOW) / 2.0
 HALO = 40
-UNIT = 16
+UNIT = 104
 MESH = pl.DeviceIdType.MESH
 OFF = 88
 
@@ -35,7 +35,7 @@
     lane = lax.broadcasted_iota(jnp.int32, p.shape, 2)
     left = jnp.where(lane == 0, 0.0, pltpu.roll(p, 1, 2))
     right = jnp.where(lane == nz - 1, 0.0, pltpu.roll(p, nz - 1, 2))
-    total = ref[:, pl.ds(r - 1, UNIT), :] + ref[:, pl.ds(r + 1, UNIT), :]
+    total = ref[:, pl.ds(r - 1, p.shape[1]), :] + ref[:, pl.ds(r + 1, p.shape[1]), :]
     total = total + (left + right)
     total = total + jnp.concatenate([zero, p[:-1]], axis=0)
     return total + jnp.concatenate([p[1:], zero], axis=0)
@@ -47,24 +47,25 @@
     last = sub == n_sub - 1
 
     def sweep(app, fn):
-        units = -(-(total_apps - app) // UNIT)
-        lo = jnp.where(first, 0, -units)
-        hi = jnp.where(last, 0, units) + rows // UNIT
+        halo = -(-(total_apps - app) // 8) * 8
+        count = rows + 2 * halo
+        begin = OFF - jnp.where(first, 0, jnp.where(last, 2 * halo, halo))
+        whole, rest = divmod(count, UNIT)
 
         def step(i, carry):
-            fn(pl.multiple_of(OFF + i * UNIT, 8))
+            fn(pl.multiple_of(begin + i * UNIT, 8), UNIT)
             return carry
 
-        lax.fori_loop(lo, hi, step, 0)
-
-    def at(ref, r):
-        return ref[:, pl.ds(r, UNIT), :]
+        lax.fori_loop(0, whole, step, 0)
+        if rest:
+            fn(pl.multiple_of(begin + whole * UNIT, 8), rest)
 
     def put(ref, r, value):
-        ref[:, pl.ds(r, UNIT), :] = value
-
-    def start(r):
-        put(src, r, at(cond, r) * at(u0, r))
+        ref[:, pl.ds(r, value.shape[1]), :] = value
+
+    def start(r, size):
+        part = pl.ds(r, size)
+        put(src, r, cond[:, part, :] * u0[:, part, :])
 
     sweep(0, start)
     fields = [u0] + list(us)
@@ -75,7 +76,8 @@
             app += 1
             a, b = w[k]
 
-            def one(r, k=k, a=a, b=b, solve=solve):
+            def one(r, size, k=k, a=a, b=b, solve=solve):
+                at = lambda ref, r: ref[:, pl.ds(r, size), :]
                 c = at(cond, r)
                 if k == 0:
                     s = at(src, r)
@@ -98,7 +100,7 @@
                     if solve < STEPS - 1:
                         put(src, r, c * new)
                     else:
-                        put(src, r, new - obs[STEPS - 1, :, pl.ds(r, UNIT), :])
+                        put(src, r, new - obs[STEPS - 1, :, pl.ds(r, size), :])
                     return
                 n = 2 * STEPS - solve
                 older = at(fields[n - 1], r)
@@ -108,7 +110,7 @@
                 else:
                     put(grad, r, at(grad, r) + add)
                 if n > 1:
-                    put(src, r, older - obs[n - 2, :, pl.ds(r, UNIT), :] + c * new)
+                    put(src, r, older - obs[n - 2, :, pl.ds(r, size), :] + c * new)
 
             if k == DEG - 1 and STEPS - 1 <= solve < 2 * STEPS - 1:
                 need_obs(2 * STEPS - 2 - solve)

time: 102 us -> 81.4 us (0.80)
  the two profiles are of different devices: /device:TPU:15 before, /device:TPU:11 now
where the time goes in v3:
time: 81.4 us; the launch traced here: 81.2 us
  Pallas kernels  74.9 us (92%)
  local copies, waits for them, and re-layouts  5.58 us (7%)
    pallas_call x1, Pallas kernels, body(): pl.pallas_call(functools.partial(whole_kernel, n_mesh, n_sub, rows), out_...  74.9 us
    unnamed x10, local copies, waits for them, and re-layouts  5.58 us

profile of v3, /device:TPU:11, one launch (start us, length us, event | category | flops | bytes accessed | tf_op | source)
XLA Modules:
  0.0 81.2 jit_solution(10822784986132049888)
XLA Ops:
  0.6 0.0 copy-start
  0.6 1.4 %copy-done = f32[1,3,2,512,128]{4,3,2,1,0:T(8,128)S(1)} copy-done((f32[1,3,2,512,128]{4,3,2,1,0:T(8,128)S(1)}, f32[1,3,2,512,128]{4,3,2,1,0:T(8,128)}, u32[]{:S(2)}) %copy-start) | copy-done | bytes 1572888
  2.0 0.0 copy-start.1
  2.0 1.0 %copy-done.1 = f32[1,2,512,128]{3,2,1,0:T(8,128)S(1)} copy-done((f32[1,2,512,128]{3,2,1,0:T(8,128)S(1)}, f32[1,2,512,128]{3,2,1,0:T(8,128)}, u32[]{:S(2)}) %copy-start.1) | copy-done | bytes 524312
  3.1 0.0 copy-start.2
  3.1 0.9 %copy-done.2 = f32[1,4,2,64,128]{4,3,2,1,0:T(8,128)S(1)} copy-done((f32[1,4,2,64,128]{4,3,2,1,0:T(8,128)S(1)}, f32[1,4,2,64,128]{4,3,2,1,0:T(8,128)}, u32[]{:S(2)}) %copy-start.2) | copy-done | bytes 262168
  4.0 0.0 copy-start.3
  4.0 0.7 copy-done.3
  4.7 74.9 %shard_map.59 = (f32[1,4,2,64,128]{4,3,2,1,0:T(8,128)S(1)}, f32[1,2,512,128]{3,2,1,0:T(8,128)S(1)}) custom-call(s32[8,8]{1,0:T(8,128)S(1)} %copy-done.3, f32[1,4,2,64,128]{4,3,2,1,0:T(8,128)S(1)} %copy-done.2, f32[1,2,512,128]{3,2,1,0:T(8,128)S(1)} %copy-done.1, f32[1,3,2,512,128]{4,3,2,1,0:T(8,128)S(1)} %copy-done), custom_call_target="tpu_custom_call" | custom-call | tf_op jit(solution)/shard_map/pallas_call | solution.py:298
  79.7 0.7 copy.8
  80.4 0.8 copy.9
Async XLA Ops:
  0.6 1.4 %copy-start = (f32[1,3,2,512,128]{4,3,2,1,0:T(8,128)S(1)}, f32[1,3,2,512,128]{4,3,2,1,0:T(8,128)}, u32[]{:S(2)}) copy-start(f32[1,3,2,512,128]{4,3,2,1,0:T(8,128)} %o_ref.1) | copy-start | bytes 4718596
  2.0 1.0 %copy-start.1 = (f32[1,2,512,128]{3,2,1,0:T(8,128)S(1)}, f32[1,2,512,128]{3,2,1,0:T(8,128)}, u32[]{:S(2)}) copy-start(f32[1,2,512,128]{3,2,1,0:T(8,128)} %u_ref.1) | copy-start | bytes 1572868
  3.1 0.9 %copy-start.2 = (f32[1,4,2,64,128]{4,3,2,1,0:T(8,128)S(1)}, f32[1,4,2,64,128]{4,3,2,1,0:T(8,128)}, u32[]{:S(2)}) copy-start(f32[1,4,2,64,128]{4,3,2,1,0:T(8,128)} %c_ref.1) | copy-start | bytes 786436
  4.0 0.7 copy-start.3
